TPU v7x, 32 devices: a whole 2x2x4 slice. The times are simulated.
32 devices in a mesh: seq: 2 (over x), mp: 4 (over z), dp: 4 (over y, core).
Axes of the slice: x: 2, y: 2, z: 4, core: 2. Of those that a mesh axis runs over, the one named last changes fastest.
Arguments:
- query: bfloat16 [2048, 4096], P(('dp', 'seq'), 'mp'), parts along dimension 0, may hold values from -6 to 6
- key: bfloat16 [2048, 4096], P(('dp', 'seq'), 'mp'), parts along dimension 0, may hold values from -6 to 6
- value: bfloat16 [2048, 4096], P(('dp', 'seq'), 'mp'), parts along dimension 0, may hold values from -6 to 6
- out_weight: bfloat16 [4096, 6144], P('seq', 'mp'), may hold values from -1.5 to 1.5
- lengths: int32 [48], P('dp'), parts along dimension 0, may hold values from 1 to 384, 512 in all
- grad_out: bfloat16 [2048, 6144], P(('dp', 'seq'), 'mp'), parts along dimension 0, may hold values from -0.29882812 to 0.29882812
Outputs:
- mixed: bfloat16 [2048, 6144], P(('dp', 'seq'), 'mp'), parts along dimension 0
- grad_query: bfloat16 [2048, 4096], P(('dp', 'seq'), 'mp'), parts along dimension 0
- grad_key: bfloat16 [2048, 4096], P(('dp', 'seq'), 'mp'), parts along dimension 0
- grad_value: bfloat16 [2048, 4096], P(('dp', 'seq'), 'mp'), parts along dimension 0
- grad_weight: bfloat16 [16384, 6144], P(('dp', 'seq'), 'mp'), parts along dimension 0
There are 4 independent parts, one for each index of `dp`. A program takes and returns all parts, laid end to end along the dimension named above; an argument that names none is the same for every part. Nothing has to cross between parts.
Inputs may be any that keep to these rules, and one draw needn't show every extreme that they name: The images lie end to end from position 0 and their lengths sum to 512.
All inputs are finite; a program needn't handle non-finite values.
Results may differ from a plain program's by a relative error of at most 0.025.
Values may be sent and summed in bfloat16 or wider, within the bound.
A program may use at most 128 MiB of HBM per device.

v0:
```python
import math

import jax
import jax.numpy as jnp
from jax import lax
from jax.sharding import PartitionSpec as P

HEAD_DIM = 128


NEG = -1e30


def image_ids(ends, first, count):
    places = first + jnp.arange(count, dtype=jnp.int32)
    return jnp.sum((places[:, None] >= ends[None, :]).astype(jnp.int32), axis=1)


def body(query, key, value, out_weight, lengths, grad_out):
    tok_rows, width = query.shape
    heads = width // HEAD_DIM
    scale = HEAD_DIM ** (-0.5)
    ends = jnp.cumsum(lengths)
    first_row = lax.axis_index("seq") * tok_rows
    query_ids = image_ids(ends, first_row, tok_rows)
    every_q, every_k, every_v = (
        lax.all_gather(query, "seq", axis=0, tiled=True),
        lax.all_gather(key, "seq", axis=0, tiled=True),
        lax.all_gather(value, "seq", axis=0, tiled=True),
    )
    seq_total = every_k.shape[0]
    block = math.gcd(512, seq_total)
    steps_all = jnp.arange(seq_total // block, dtype=jnp.int32)
    local_q = query.reshape(tok_rows, heads, HEAD_DIM)
    local_k = key.reshape(tok_rows, heads, HEAD_DIM)
    local_v = value.reshape(tok_rows, heads, HEAD_DIM)

    def key_block(index):
        begin = index * block
        keys = lax.dynamic_slice_in_dim(every_k, begin, block, 0).reshape(block, heads, HEAD_DIM)
        vals = lax.dynamic_slice_in_dim(every_v, begin, block, 0).reshape(block, heads, HEAD_DIM)
        return (keys, vals, image_ids(ends, begin, block))

    def masked_scores(left, right, left_ids, right_ids):
        same = left_ids[:, None] == right_ids[None, :]
        score = jnp.einsum("qhd,khd->hqk", left, right, preferred_element_type=jnp.float32) * scale
        return (jnp.where(same[None], score, NEG), same)

    def forward_step(carry, index):
        keys, vals, key_ids = key_block(index)
        top, total, acc = carry
        score, same = masked_scores(local_q, keys, query_ids, key_ids)
        new_top = jnp.maximum(top, jnp.max(score, axis=2))
        weights = jnp.where(same[None], jnp.exp(score - new_top[:, :, None]), 0.0)
        fade = jnp.exp(top - new_top)
        total = total * fade + jnp.sum(weights, axis=2)
        acc = acc * fade[:, :, None] + jnp.einsum(
            "hqk,khd->hqd", weights.astype(jnp.bfloat16), vals, preferred_element_type=jnp.float32
        )
        carry = (new_top, total, acc)
        return (carry, None)

    start_state = (
        jnp.full((heads, tok_rows), NEG, jnp.float32),
        jnp.zeros((heads, tok_rows), jnp.float32),
        jnp.zeros((heads, tok_rows, HEAD_DIM), jnp.float32),
    )
    (top, total, acc), unused = lax.scan(forward_step, start_state, steps_all)
    attn_local = (acc / total[:, :, None]).astype(jnp.bfloat16)
    stats = top + jnp.log(total)
    attention = attn_local.transpose(1, 0, 2).reshape(tok_rows, width)
    every_heads = lax.all_gather(attention, "mp", axis=1, tiled=True)
    weight_full = lax.all_gather(out_weight, "seq", axis=0, tiled=True)
    mixed = jnp.dot(every_heads, weight_full, preferred_element_type=jnp.float32).astype(
        jnp.bfloat16
    )
    rows = weight_full
    d_attention = (
        lax.psum_scatter(
            lax.dot_general(
                rows, grad_out, (((1,), (1,)), ((), ())), preferred_element_type=jnp.float32
            ).astype(jnp.bfloat16),
            "mp",
            scatter_dimension=0,
            tiled=True,
        )
        .astype(jnp.float32)
        .T.astype(jnp.bfloat16)
    )
    token_heads = lax.all_to_all(every_heads, "seq", split_axis=1, concat_axis=0, tiled=True)
    rows = token_heads
    grad_weight = lax.dot_general(
        rows,
        lax.all_gather(grad_out, "seq", axis=0, tiled=True),
        (((0,), (0,)), ((), ())),
        preferred_element_type=jnp.float32,
    ).astype(jnp.bfloat16)
    d_local = d_attention.reshape(tok_rows, heads, HEAD_DIM)
    deltas = jnp.sum(
        d_local.astype(jnp.float32)
        * attention.reshape(tok_rows, heads, HEAD_DIM).astype(jnp.float32),
        axis=2,
    ).T

    def query_step(summed, index):
        keys, vals, key_ids = key_block(index)
        score, same = masked_scores(local_q, keys, query_ids, key_ids)
        prob = jnp.exp(score - stats[:, :, None])
        d_p = jnp.einsum("qhd,khd->hqk", d_local, vals, preferred_element_type=jnp.float32)
        d_score = (prob * (d_p - deltas[:, :, None])).astype(jnp.bfloat16)
        summed = summed + jnp.einsum(
            "hqk,khd->qhd", d_score, keys, preferred_element_type=jnp.float32
        )
        return (summed, None)

    dq_sum, unused = lax.scan(
        query_step, jnp.zeros((tok_rows, heads, HEAD_DIM), jnp.float32), steps_all
    )
    grad_query = (dq_sum * scale).reshape(tok_rows, width).astype(jnp.bfloat16)
    d_piece = lax.all_gather(d_attention.astype(jnp.float32), "seq", axis=0, tiled=True)
    stat_piece = lax.all_gather(stats.T, "seq", axis=0, tiled=True)
    delta_piece = lax.all_gather(deltas.T, "seq", axis=0, tiled=True)
    count = d_piece.shape[0]
    far_q = every_q.reshape(count, heads, HEAD_DIM)
    far_ids = image_ids(ends, jnp.int32(0), count)
    d_far = d_piece.astype(jnp.bfloat16).reshape(count, heads, HEAD_DIM)
    score, same = masked_scores(far_q, local_k, far_ids, query_ids)
    prob = jnp.exp(score - stat_piece.T[:, :, None])
    acc_v = jnp.einsum(
        "hqk,qhd->khd", prob.astype(jnp.bfloat16), d_far, preferred_element_type=jnp.float32
    )
    d_p = jnp.einsum("qhd,khd->hqk", d_far, local_v, preferred_element_type=jnp.float32)
    d_score = (prob * (d_p - delta_piece.T[:, :, None])).astype(jnp.bfloat16)
    acc_k = jnp.einsum("hqk,qhd->khd", d_score, far_q, preferred_element_type=jnp.float32)
    grad_key = (acc_k * scale).reshape(tok_rows, width).astype(jnp.bfloat16)
    grad_value = acc_v.reshape(tok_rows, width).astype(jnp.bfloat16)
    return (mixed, grad_query, grad_key, grad_value, grad_weight)


def solution(mesh):
    placed = (
        P(("dp", "seq"), "mp"),
        P(("dp", "seq"), "mp"),
        P(("dp", "seq"), "mp"),
        P("seq", "mp"),
        P("dp"),
        P(("dp", "seq"), "mp"),
    )
    return jax.shard_map(
        body,
        mesh=mesh,
        in_specs=placed,
        out_specs=(
            P(("dp", "seq"), "mp"),
            P(("dp", "seq"), "mp"),
            P(("dp", "seq"), "mp"),
            P(("dp", "seq"), "mp"),
            P(("dp", "seq"), "mp"),
        ),
        check_vma=False,
    )
```

profile of v0, /device:TPU:0, one launch (start us, length us, event | category | flops | bytes accessed | tf_op | source)
XLA Modules:
  0.0 414.6 jit_solution(12352164706959780977)
XLA Ops:
  7.2 0.7 all-gather.14.cloned.1.call-update
  8.0 0.2 copy-done.2
  8.2 1.0 copy.44
  9.3 155.5 %all-gather.14.cloned.1.call-done = bf16[4096,1536]{1,0:T(8,128)(2,1)} async-done(((bf16[2048,1536]{1,0:T(8,128)(2,1)}), bf16[4096,1536]{1,0:T(8,128)(2,1)}) %all-gather.14.cloned.1.call-update) | async-done | bytes 12582928 | tf_op jit(solution)/shard_map/all_gather | solution.py:73
  164.8 9.4 %convolution_convert_fusion.1 = bf16[4096,256]{1,0:T(8,128)(2,1)} fusion(bf16[4096,1536]{1,0:T(8,128)(2,1)} %all-gather.14.cloned.1.call-done, bf16[256,1536]{1,0:T(8,128)(2,1)S(1)} %copy-done.5), kind=kOutput, calls=%fused_computation.1 | convolution fusion | flops 3222274048 | bytes 15466496 | tf_op jit(solution)/shard_map/dot_general | solution.py:80
  174.3 0.5 all-gather.10.cloned.1.call-update
  174.9 1.0 copy.50
  176.5 11.7 %all-gather.8.cloned.1.call-done = bf16[512,1024]{0,1:T(8,128)(2,1)} async-done(((bf16[256,1024]{0,1:T(8,128)(2,1)}), bf16[512,1024]{0,1:T(8,128)(2,1)}) %all-gather.8.cloned.1.call-update) | async-done | bytes 1048592 | tf_op jit(solution)/shard_map/all_gather | solution.py:28
  188.2 4.1 fusion.3
  192.3 42.1 %reduce-scatter.2.cloned.1.call-done = bf16[1024,256]{1,0:T(8,128)(2,1)} async-done(((bf16[4096,256]{1,0:T(8,128)(2,1)}), bf16[1024,256]{1,0:T(8,128)(2,1)}) %reduce-scatter.2.cloned.1.call-update) | async-done | bytes 524304 | tf_op jit(solution)/shard_map/reduce_scatter | solution.py:79
  234.5 3.7 fusion
  238.3 18.3 %all-gather.10.cloned.1.call-done = bf16[512,1024]{1,0:T(8,128)(2,1)} async-done(((bf16[256,1024]{1,0:T(8,128)(2,1)}), bf16[512,1024]{1,0:T(8,128)(2,1)}) %all-gather.10.cloned.1.call-update) | async-done | bytes 1048592 | tf_op jit(solution)/shard_map/all_gather | solution.py:29
  256.6 1.5 copy.47
  258.1 4.4 %multiply_reduce_fusion = (f32[256,8]{0,1:T(8,128)S(1)}, bf16[256,8,128]{0,2,1:T(8,128)(2,1)}) fusion(bf16[1024,256]{1,0:T(8,128)(2,1)S(1)} %copy-done.6, f32[256,8]{0,1:T(8,128)S(1)} %get-tuple-element.83, bf16[512,8,128]{0,2,1:T(8,128)(2,1)S(1)} %bitcast.91, f32[8,256,512]{2,1,0:T(8,128)} %get-tuple-element.86, f32[8,256]{1,0:T(8,128)S(1)} %broadcast_maximum_fusion, ...), kind=kOutput, calls=%fused_computation.27 | convolution fusion | flops 275511296 | bytes 6455296 | tf_op jit(solution)/shard_map/while/body/eval_jaxpr/hqk,khd->hqd/dot_general | solution.py:57
  262.6 0.7 all-gather.20.cloned.1.call-update
  263.5 16.4 %all-gather.16.cloned.1.call-done = bf16[512,1024]{0,1:T(8,128)(2,1)} async-done(((bf16[256,1024]{0,1:T(8,128)(2,1)}), bf16[512,1024]{0,1:T(8,128)(2,1)}) %all-gather.16.cloned.1.call-update) | async-done | bytes 1048592 | tf_op jit(solution)/shard_map/all_gather | solution.py:27
  279.9 3.9 fusion.32
  283.8 4.4 %all_gather.32 = f32[512,8]{0,1:T(8,128)S(1)} all-gather(f32[256,8]{0,1:T(8,128)S(1)} %get-tuple-element.82), channel_id=1, replica_groups=mesh['seq'=2,'mp'=4,'dp'=4] {'seq'}, dimensions={0}, use_global_device_ids=true | all-gather | bytes 24576 | tf_op jit(solution)/shard_map/all_gather | solution.py:121
  288.2 4.5 %all_gather.34 = f32[512,8]{0,1:T(8,128)S(1)} all-gather(f32[256,8]{0,1:T(8,128)S(1)} %get-tuple-element.87), channel_id=1, replica_groups=mesh['seq'=2,'mp'=4,'dp'=4] {'seq'}, dimensions={0}, use_global_device_ids=true | all-gather | bytes 24576 | tf_op jit(solution)/shard_map/all_gather | solution.py:122
  292.7 5.4 %fusion.22 = bf16[8,256,128]{1,2,0:T(8,128)(2,1)} fusion(bf16[512,8,128]{0,2,1:T(8,128)(2,1)S(1)} %bitcast.94, f32[8,256,512]{2,1,0:T(8,128)} %get-tuple-element.86, bf16[256,8,128]{0,2,1:T(8,128)(2,1)} %bitcast.98, bf16[512,8,128]{0,2,1:T(8,128)(2,1)S(1)} %bitcast.92, f32[8,256]{1,0:T(8,128)S(1)} %bitcast.106, f32[8,256]{1,0:T(8,128)S(1)} %log_add_fusion, ...), kind=kOutput, calls=%fused_computation.25 | convolution fusion | flops 543686656 | bytes 7487488 | tf_op jit(solution)/shard_map/while/body/eval_jaxpr/hqk,khd->qhd/dot_general | solution.py:111
  298.1 2.0 copy.56
  300.1 2.6 all-gather.18.cloned.1.call-done
  302.8 4.7 %fusion.21 = bf16[8,256,128]{1,2,0:T(8,128)(2,1)S(1)} fusion(bf16[512,8,128]{0,2,1:T(8,128)(2,1)S(1)} %bitcast.96, f32[8,512,256]{2,1,0:T(8,128)} %fusion.32, bf16[512,8,128]{0,2,1:T(8,128)(2,1)} %bitcast.109, f32[8,512]{1,0:T(8,128)S(1)} %bitcast.105, f32[8,512]{1,0:T(8,128)S(1)} %bitcast.103, pred[512,256]{1,0:T(8,128)(4,1)S(1)} %broadcast_compare_fusion, ...), kind=kOutput, calls=%fused_computation.24 | convolution fusion | flops 543686656 | bytes 7503872 | tf_op jit(solution)/shard_map/hqk,qhd->khd/dot_general | solution.py:134
  307.5 1.0 copy.57
  308.5 3.0 fusion.23
  311.5 1.0 copy.58
  312.5 38.5 %all-gather.12.cloned.1.call-done = bf16[256,4096]{0,1:T(8,128)(2,1)} async-done(((bf16[256,1024]{0,1:T(8,128)(2,1)}), bf16[256,4096]{0,1:T(8,128)(2,1)}) %all-gather.12.cloned.1.call-update) | async-done | bytes 2097168 | tf_op jit(solution)/shard_map/all_gather | solution.py:72
  350.9 5.0 %all-to-all-start = ((bf16[256,2,2048]{0,2,1:T(8,128)(2,1)}), bf16[256,2,2048]{0,2,1:T(8,128)(2,1)}, u32[]{:S(2)}, u32[]{:S(2)}) async-start(bf16[256,2,2048]{0,2,1:T(8,128)(2,1)} %bitcast.89), calls=%async_computation.1 | async-start | bytes 4194304 | tf_op jit(solution)/shard_map/all_to_all | solution.py:90
  356.0 8.2 %convolution_convert_fusion.2 = bf16[256,1536]{1,0:T(8,128)(2,1)} fusion(bf16[256,4096]{0,1:T(8,128)(2,1)S(1)} %copy-done, bf16[4096,1536]{1,0:T(8,128)(2,1)} %all-gather.14.cloned.1.call-done), kind=kOutput, calls=%fused_computation.11 | convolution fusion | flops 3221618688 | bytes 15466496 | tf_op jit(solution)/shard_map/dot_general | solution.py:74
  364.1 33.9 %all-to-all-done = bf16[256,2,2048]{0,2,1:T(8,128)(2,1)} async-done(((bf16[256,2,2048]{0,2,1:T(8,128)(2,1)}), bf16[256,2,2048]{0,2,1:T(8,128)(2,1)}, u32[]{:S(2)}, u32[]{:S(2)}) %all-to-all-start) | async-done | bytes 2097184 | tf_op jit(solution)/shard_map/all_to_all | solution.py:90
  398.0 2.9 copy.55
  401.0 6.8 %convolution_convert_fusion = bf16[2048,1536]{1,0:T(8,128)(2,1)} fusion(bf16[512,2048]{1,0:T(8,128)(2,1)S(1)} %bitcast.90, bf16[512,1536]{1,0:T(8,128)(2,1)} %all-gather.20.cloned.1.call-done), kind=kOutput, calls=%fused_computation | convolution fusion | flops 3224371200 | bytes 9961472 | tf_op jit(solution)/shard_map/dot_general | solution.py:92
  (40 shorter events, 1.1 us)
Async XLA Ops:
  7.2 1.0 copy-start.2
  7.2 157.7 %copy-start.5 = (bf16[256,1536]{1,0:T(8,128)(2,1)S(1)}, bf16[256,1536]{1,0:T(8,128)(2,1)}, u32[]{:S(2)}) copy-start(bf16[256,1536]{1,0:T(8,128)(2,1)} %param.11) | copy-start | bytes 2359300
  7.2 157.6 %all-gather.14.cloned.1.call-start = ((), (), s32[]{:S(2)}) async-start(), calls=%async_computation.5 | async-start | bytes 18874368 | tf_op jit(solution)/shard_map/all_gather | solution.py:73
  7.9 180.3 %all-gather.8.cloned.1.call-start = ((), (), s32[]{:S(2)}) async-start(), calls=%async_computation.2 | async-start | bytes 1572864 | tf_op jit(solution)/shard_map/all_gather | solution.py:28
  9.2 165.6 %copy-start.1 = (bf16[256,1024]{1,0:T(8,128)(2,1)S(1)}, bf16[256,1024]{1,0:T(8,128)(2,1)}, u32[]{:S(2)}) copy-start(bf16[256,1024]{1,0:T(8,128)(2,1)} %param.6) | copy-start | bytes 1572868
  9.2 225.2 %reduce-scatter.2.cloned.1.call-start = ((), (), s32[]{:S(2)}) async-start(), calls=%async_computation.6 | async-start | bytes 2621440 | tf_op jit(solution)/shard_map/reduce_scatter | solution.py:79
  174.2 1.7 copy-start.8
  174.3 82.3 %all-gather.10.cloned.1.call-start = ((), (), s32[]{:S(2)}) async-start(), calls=%async_computation.3 | async-start | bytes 1572864 | tf_op jit(solution)/shard_map/all_gather | solution.py:29
  174.8 105.1 %all-gather.16.cloned.1.call-start = ((), (), s32[]{:S(2)}) async-start(), calls=%async_computation.7 | async-start | bytes 1572864 | tf_op jit(solution)/shard_map/all_gather | solution.py:27
  175.9 126.8 %all-gather.18.cloned.1.call-start = ((), (), s32[]{:S(2)}) async-start(), calls=%async_computation.8 | async-start | bytes 1572864 | tf_op jit(solution)/shard_map/all_gather | solution.py:120
  234.5 23.6 %copy-start.6 = (bf16[1024,256]{1,0:T(8,128)(2,1)S(1)}, bf16[1024,256]{1,0:T(8,128)(2,1)}, u32[]{:S(2)}) copy-start(bf16[1024,256]{1,0:T(8,128)(2,1)} %reduce-scatter.2.cloned.1.call-done) | copy-start | bytes 1572868
  234.5 116.5 %all-gather.12.cloned.1.call-start = ((), (), s32[]{:S(2)}) async-start(), calls=%async_computation.4 | async-start | bytes 2621440 | tf_op jit(solution)/shard_map/all_gather | solution.py:72
  262.5 30.2 %copy-start.3 = (bf16[512,1024]{0,1:T(8,128)(2,1)S(1)}, bf16[512,1024]{0,1:T(8,128)(2,1)}, u32[]{:S(2)}) copy-start(bf16[512,1024]{0,1:T(8,128)(2,1)} %all-gather.8.cloned.1.call-done) | copy-start | bytes 3145732
  262.6 138.4 %all-gather.20.cloned.1.call-start = ((), (), s32[]{:S(2)}) async-start(), calls=%async_computation.9 | async-start | bytes 2359296 | tf_op jit(solution)/shard_map/all_gather | solution.py:94
  292.7 10.1 %copy-start.4 = (bf16[512,1024]{0,1:T(8,128)(2,1)S(1)}, bf16[512,1024]{0,1:T(8,128)(2,1)}, u32[]{:S(2)}) copy-start(bf16[512,1024]{0,1:T(8,128)(2,1)} %all-gather.16.cloned.1.call-done) | copy-start | bytes 3145732
  302.8 5.7 %copy-start.7 = (bf16[512,1024]{0,1:T(8,128)(2,1)S(1)}, bf16[512,1024]{0,1:T(8,128)(2,1)}, u32[]{:S(2)}) copy-start(bf16[512,1024]{0,1:T(8,128)(2,1)} %all-gather.18.cloned.1.call-done) | copy-start | bytes 3145732
  350.9 5.0 %copy-start = (bf16[256,4096]{0,1:T(8,128)(2,1)S(1)}, bf16[256,4096]{0,1:T(8,128)(2,1)}, u32[]{:S(2)}) copy-start(bf16[256,4096]{0,1:T(8,128)(2,1)} %all-gather.12.cloned.1.call-done) | copy-start | bytes 6291460
  350.9 47.1 %all-to-all-start = ((bf16[256,2,2048]{0,2,1:T(8,128)(2,1)}), bf16[256,2,2048]{0,2,1:T(8,128)(2,1)}, u32[]{:S(2)}, u32[]{:S(2)}) async-start(bf16[256,2,2048]{0,2,1:T(8,128)(2,1)} %bitcast.89), calls=%async_computation.1 | async-start | bytes 4194304 | tf_op jit(solution)/shard_map/all_to_all | solution.py:90
Sparse Core Ops, SparseCore 0:
  9.6 155.2 all-gather.13
  166.9 21.2 all-gather.7
  190.5 43.8 reduce-scatter.1
  235.9 20.5 all-gather.9
  258.6 21.2 all-gather.15
  281.4 21.3 all-gather.17
  305.0 45.9 all-gather.11
  352.6 42.9 all-gather.19
where the time goes:
time: 415 us
  waiting for transfers between devices  321 us (77%)
  matrix products  49.9 us (12%)
  between operations  14.3 us (3%)
  local copies, waits for them, and re-layouts  10.7 us (3%)
  blocking collectives  8.89 us (2%)
  starting transfers between devices  5.32 us (1%)
  other arithmetic  4.41 us (1%)
    all_gather x1, waiting for transfers between devices, body(): weight_full = lax.all_gather(out_weight, 'seq', axis=0, tiled=True)  156 us
    reduce_scatter x1, waiting for transfers between devices, body(): lax.psum_scatter(lax.dot_general(rows, grad_out, (((1,), (1,)), ((), ()))...  42.1 us
    all_gather x1, waiting for transfers between devices, body(): every_heads = lax.all_gather(attention, 'mp', axis=1, tiled=True)  38.5 us
    all_to_all x1, waiting for transfers between devices, body(): lax.all_to_all(every_heads, 'seq', split_axis=1, concat_axis=0, tiled=True)  33.9 us
    all_gather x1, waiting for transfers between devices, body(): lax.all_gather(value, 'seq', axis=0, tiled=True)  18.3 us
    all_gather x1, waiting for transfers between devices, body(): lax.all_gather(query, 'seq', axis=0, tiled=True)  16.4 us
    all_gather x1, waiting for transfers between devices, body(): lax.all_gather(key, 'seq', axis=0, tiled=True)  11.7 us
    dot_general x1, matrix products, body(): lax.dot_general(rows, grad_out, (((1,), (1,)), ((), ())), preferred_eleme...  9.39 us
  transfers between devices with their start and end apart: 9, of which 8 were waited for; matrix products, arithmetic and copies ran while one was open for 14% of the time, Pallas kernels for 0%

commit v1 on v0

--- a/solution.py
+++ b/solution.py
@@ -3,11 +3,14 @@
 import jax
 import jax.numpy as jnp
 from jax import lax
+from jax.experimental import pallas as pl
+from jax.experimental.pallas import tpu as pltpu
 from jax.sharding import PartitionSpec as P
 
 HEAD_DIM = 128
 
 
+HEADS_IN_ALL = 32
 NEG = -1e30
 
 
@@ -137,6 +140,172 @@
     return (mixed, grad_query, grad_key, grad_value, grad_weight)
 
 
+def masked_softmax(q, k, row_ids, col_ids):
+    score = lax.dot_general(q, k, (((1,), (1,)), ((), ())), preferred_element_type=jnp.float32)
+    score = score * HEAD_DIM ** (-0.5)
+    same = row_ids == col_ids
+    score = jnp.where(same, score, NEG)
+    top = jnp.max(score, axis=1, keepdims=True)
+    weights = jnp.where(same, jnp.exp(score - top), 0.0)
+    return weights, jnp.sum(weights, axis=1, keepdims=True)
+
+
+def joined(own, far):
+    return jnp.concatenate([own[...], far[...]], axis=0)
+
+
+def forward_kernel(me, rid, cid, qo, qf, ko, kf, vo, vf, out):
+    weights, total = masked_softmax(joined(qo, qf), joined(ko, kf), rid[...], cid[...])
+    acc = jnp.dot(weights.astype(jnp.bfloat16), joined(vo, vf), preferred_element_type=jnp.float32)
+    out[...] = (acc / total).astype(jnp.bfloat16)
+
+
+def backward_kernel(me, rid, cid, qo, qf, ko, kf, vo, vf, att, datt, *outs):
+    q, k, v = joined(qo, qf), joined(ko, kf), joined(vo, vf)
+    d_out = datt[...]
+    weights, total = masked_softmax(q, k, rid[...], cid[...])
+    prob = weights * (1.0 / total)
+    delta = jnp.sum(
+        d_out.astype(jnp.float32) * att[...].astype(jnp.float32), axis=1, keepdims=True
+    )
+    d_v = lax.dot_general(
+        prob.astype(jnp.bfloat16), d_out, (((0,), (0,)), ((), ())),
+        preferred_element_type=jnp.float32,
+    )
+    d_p = lax.dot_general(d_out, v, (((1,), (1,)), ((), ())), preferred_element_type=jnp.float32)
+    d_score = (prob * (d_p - delta)).astype(jnp.bfloat16)
+    scale = HEAD_DIM ** (-0.5)
+    d_q = jnp.dot(d_score, k, preferred_element_type=jnp.float32) * scale
+    d_k = lax.dot_general(
+        d_score, q, (((0,), (0,)), ((), ())), preferred_element_type=jnp.float32
+    ) * scale
+    rows = qo.shape[0]
+    for grad, own, far in ((d_q, 0, 1), (d_k, 2, 3), (d_v, 4, 5)):
+        outs[own][...] = grad[:rows].astype(jnp.bfloat16)
+        outs[far][...] = grad[rows:].astype(jnp.bfloat16)
+
+
+def attention_call(kernel, me, ids, pairs, extra, split_out):
+    rows = pairs[0][1].shape[0]
+    width = pairs[0][1].shape[1]
+    heads = width // HEAD_DIM
+    own = pl.BlockSpec((rows, HEAD_DIM), lambda h, me: (0, me[0] * heads + h))
+    far = pl.BlockSpec((rows, HEAD_DIM), lambda h, me: (0, h))
+    both = pl.BlockSpec((2 * rows, HEAD_DIM), lambda h, me: (0, h))
+    whole = [
+        pl.BlockSpec((2 * rows, 1), lambda h, me: (0, 0)),
+        pl.BlockSpec((1, 2 * rows), lambda h, me: (0, 0)),
+    ]
+    if split_out:
+        out_specs = [far] * 6
+        out_shape = [jax.ShapeDtypeStruct((rows, width), jnp.bfloat16)] * 6
+    else:
+        out_specs = both
+        out_shape = jax.ShapeDtypeStruct((2 * rows, width), jnp.bfloat16)
+    matmuls = 5 if split_out else 2
+    cells = 4 * rows * rows * heads
+    return pl.pallas_call(
+        kernel,
+        grid_spec=pltpu.PrefetchScalarGridSpec(
+            num_scalar_prefetch=1,
+            grid=(heads,),
+            in_specs=whole + [own, far] * 3 + [both] * len(extra),
+            out_specs=out_specs,
+        ),
+        out_shape=out_shape,
+        cost_estimate=pl.CostEstimate(
+            flops=cells * 2 * HEAD_DIM * matmuls * 4,
+            bytes_accessed=2 * rows * width * 2 * (4 + len(extra) + (3 if split_out else 0)),
+            transcendentals=cells,
+        ),
+        compiler_params=pltpu.CompilerParams(vmem_limit_bytes=48 << 20),
+    )(me, ids[:, None], ids[None, :], *[a for pair in pairs for a in pair], *extra)
+
+
+def dot_f32(a, b, left, right):
+    return lax.dot_general(a, b, (((left,), (right,)), ((), ())), preferred_element_type=jnp.float32)
+
+
+def paired_body(query, key, value, out_weight, lengths, grad_out):
+    rows, width = query.shape
+    half = width // 2
+    groups = lax.axis_size("mp")
+    side = groups // 2
+    me = lax.axis_index("seq")
+    swap = lambda a: lax.ppermute(a, "seq", [(0, 1), (1, 0)])
+    first = me == 0
+    ends = jnp.cumsum(lengths)
+    ids = jnp.concatenate(
+        [image_ids(ends, me * rows, rows), image_ids(ends, (1 - me) * rows, rows)]
+    )
+
+    def away(a):
+        return lax.dynamic_slice_in_dim(a, (1 - me) * half, half, 1)
+
+    far_q, far_k, far_v = swap(away(query)), swap(away(key)), swap(away(value))
+    far_go = swap(grad_out)
+    features = out_weight.shape[1]
+    weight = out_weight.reshape(side, 2, half, features)
+    w_mine = lax.dynamic_index_in_dim(weight, me, 1, keepdims=False).reshape(side * half, features)
+    w_away = lax.dynamic_index_in_dim(weight, 1 - me, 1, keepdims=False).reshape(
+        side * half, features
+    )
+
+    bf = jnp.bfloat16
+    cross_own = swap(dot_f32(grad_out, w_away, 1, 1).astype(bf))
+    keep_own = dot_f32(grad_out, w_mine, 1, 1).astype(bf)
+    cross_far = swap(dot_f32(far_go, w_away, 1, 1).astype(bf))
+    keep_far = dot_f32(far_go, w_mine, 1, 1).astype(bf)
+    keep = jnp.concatenate([keep_own, keep_far], 0).reshape(2 * rows, side, half)
+    got = jnp.concatenate([cross_far, cross_own], 0).reshape(2 * rows, side, half)
+    keep, got = keep.transpose(1, 0, 2), got.transpose(1, 0, 2)
+    parts = jnp.concatenate([jnp.where(first, keep, got), jnp.where(first, got, keep)], 0)
+    d_attention = lax.psum_scatter(
+        parts.reshape(groups * 2 * rows, half), "mp", scatter_dimension=0, tiled=True
+    )
+
+    pairs = ((query, far_q), (key, far_k), (value, far_v))
+    where_me = jnp.reshape(me, (1,)).astype(jnp.int32)
+    attention = attention_call(forward_kernel, where_me, ids, pairs, (), False)
+    every = lax.all_gather(attention, "mp", axis=0, tiled=False)
+    mine = lax.dynamic_slice_in_dim(every, me * side, side, 0)
+    theirs = swap(lax.dynamic_slice_in_dim(every, (1 - me) * side, side, 0))
+
+    def beside(a, b):
+        return jnp.stack([jnp.where(first, a, b), jnp.where(first, b, a)], 1)
+
+    mine_own, mine_far = mine[:, :rows], mine[:, rows:]
+    their_own, their_far = theirs[:, rows:], theirs[:, :rows]
+    att_own = beside(mine_own, their_own)
+    att_far = beside(mine_far, their_far)
+
+    def project(att):
+        return lax.dot_general(
+            att, weight, (((0, 1, 3), (0, 1, 2)), ((), ())), preferred_element_type=jnp.float32
+        )
+
+    other = swap(project(att_far).astype(bf))
+    mixed = (project(att_own) + other.astype(jnp.float32)).astype(bf)
+    att_all = jnp.concatenate([att_own, att_far], 2)
+    go_all = jnp.concatenate([grad_out, far_go], 0)
+    grad_weight = lax.dot_general(
+        att_all, go_all, (((2,), (0,)), ((), ())), preferred_element_type=jnp.float32
+    ).astype(bf).reshape(out_weight.shape)
+
+    grads = attention_call(
+        backward_kernel, where_me, ids, pairs, (attention, d_attention), True
+    )
+
+    def home(own, far):
+        got = swap(far)
+        return jnp.concatenate([jnp.where(first, own, got), jnp.where(first, got, own)], 1)
+
+    grad_query = home(grads[0], grads[1])
+    grad_key = home(grads[2], grads[3])
+    grad_value = home(grads[4], grads[5])
+    return (mixed, grad_query, grad_key, grad_value, grad_weight)
+
+
 def solution(mesh):
     placed = (
         P(("dp", "seq"), "mp"),
@@ -146,8 +315,10 @@
         P("dp"),
         P(("dp", "seq"), "mp"),
     )
+    heads_here = HEADS_IN_ALL // mesh.shape["mp"]
+    paired = mesh.shape["seq"] == 2 and mesh.shape["mp"] % 2 == 0 and heads_here % 2 == 0
     return jax.shard_map(
-        body,
+        paired_body if paired else body,
         mesh=mesh,
         in_specs=placed,
         out_specs=(

time: 415 us -> 165 us (0.40)
  waiting for transfers between devices: 321 us -> 76.3 us
  matrix products: 49.9 us -> 26.8 us
  Pallas kernels: 0 us -> 12.4 us
  starting transfers between devices: 5.32 us -> 15.6 us
  blocking collectives: 8.89 us -> 0 us
    all_gather x7 -> x1, waiting for transfers between devices: 243 us -> 3.88 us  [paired_body(): every = lax.all_gather(attention, 'mp', axis=0, tiled=False)]
    ppermute x0 -> x11, waiting for transfers between devices: none -> 69.2 us  [paired_body(): swap = lambda a: lax.ppermute(a, 'seq', [(0, 1), (1, 0)])]
    reduce_scatter x1, waiting for transfers between devices: 42.1 us -> 3.14 us  [paired_body(): lax.psum_scatter(parts.reshape(groups * 2 * rows, half), 'mp', scatter_di...]
    all_to_all x1 -> x0, waiting for transfers between devices: 33.9 us -> none  [body(): lax.all_to_all(every_heads, 'seq', split_axis=1, concat_axis=0, tiled=True)]
    dot_general x9 -> x7, matrix products: 49.9 us -> 26.8 us  [the longest x2 11.4 us: project(): lax.dot_general(att, weight, (((0, 1, 3), (0, 1, 2)), ((), ())), preferre...]
    ppermute x0 -> x11, starting transfers between devices: none -> 15.5 us  [paired_body(): swap = lambda a: lax.ppermute(a, 'seq', [(0, 1), (1, 0)])]
    pallas_call x0 -> x2, Pallas kernels: none -> 12.4 us  [attention_call(): pl.pallas_call(kernel, grid_spec=pltpu.PrefetchScalarGridSpec(num_scalar_...]
    all_gather x2 -> x0, blocking collectives: 8.89 us -> none  [the longest x1 4.54 us: body(): delta_piece = lax.all_gather(deltas.T, 'seq', axis=0, tiled=True)]
  transfers between devices with their start and end apart: 9 -> 13, of which waited for: 8 -> 10; matrix products, arithmetic and copies ran while one was open for 14% -> 24% of each run, Pallas kernels for 0% -> 5%
where the time goes in v1:
time: 165 us
  waiting for transfers between devices  76.3 us (46%)
  matrix products  26.8 us (16%)
  starting transfers between devices  15.6 us (9%)
  between operations  14.2 us (9%)
  Pallas kernels  12.4 us (8%)
  local copies, waits for them, and re-layouts  12 us (7%)
  other arithmetic  7.38 us (4%)
    ppermute x11, waiting for transfers between devices, paired_body(): swap = lambda a: lax.ppermute(a, 'seq', [(0, 1), (1, 0)])  69.2 us
    ppermute x11, starting transfers between devices, paired_body(): swap = lambda a: lax.ppermute(a, 'seq', [(0, 1), (1, 0)])  15.5 us
    pallas_call x2, Pallas kernels, attention_call(): pl.pallas_call(kernel, grid_spec=pltpu.PrefetchScalarGridSpec(num_scalar_...  12.4 us
    dot_general x2, matrix products, project(): lax.dot_general(att, weight, (((0, 1, 3), (0, 1, 2)), ((), ())), preferre...  11.4 us
    dot_general x4, matrix products, dot_f32(): lax.dot_general(a, b, (((left,), (right,)), ((), ())), preferred_element_...  8.86 us
    dot_general x1, matrix products, paired_body(): lax.dot_general(att_all, go_all, (((2,), (0,)), ((), ())), preferred_elem...  6.63 us
    unnamed x25, local copies, waits for them, and re-layouts  4.24 us
    all_gather x1, waiting for transfers between devices, paired_body(): every = lax.all_gather(attention, 'mp', axis=0, tiled=False)  3.88 us
  transfers between devices with their start and end apart: 13, of which 10 were waited for; matrix products, arithmetic and copies ran while one was open for 24% of the time, Pallas kernels for 5%

profile of v1, /device:TPU:0, one launch (start us, length us, event | category | flops | bytes accessed | tf_op | source)
XLA Modules:
  0.0 164.8 jit_solution(8644101520647236568)
XLA Ops:
  8.2 3.0 %collective-permute-start = (bf16[256,512]{1,0:T(8,128)(2,1)S(1)}, bf16[256,512]{1,0:T(8,128)(2,1)S(1)}, u32[]{:S(2)}, u32[]{:S(2)}) collective-permute-start(bf16[256,512]{1,0:T(8,128)(2,1)S(1)} %constant_dynamic-slice_fusion.5), channel_id=1, source_target_pairs={{0,16},{16,0},{1,17},{17,1},{2,18},{18,2},{3,19},{19,3},{4,20},{20... | collective-permute-start | bytes 786440 | tf_op jit(solution)/shard_map/ppermute | solution.py:235
  13.2 2.1 %collective-permute-start.2 = (bf16[256,512]{1,0:T(8,128)(2,1)S(1)}, bf16[256,512]{1,0:T(8,128)(2,1)S(1)}, u32[]{:S(2)}, u32[]{:S(2)}) collective-permute-start(bf16[256,512]{1,0:T(8,128)(2,1)S(1)} %constant_dynamic-slice_fusion.3), channel_id=1, source_target_pairs={{0,16},{16,0},{1,17},{17,1},{2,18},{18,2},{3,19},{19,3},{4,20},{20... | collective-permute-start | bytes 786440 | tf_op jit(solution)/shard_map/ppermute | solution.py:235
  16.4 1.9 %collective-permute-done.qf = bf16[256,512]{1,0:T(8,128)(2,1)S(1)} collective-permute-done((bf16[256,512]{1,0:T(8,128)(2,1)S(1)}, bf16[256,512]{1,0:T(8,128)(2,1)S(1)}, u32[]{:S(2)}, u32[]{:S(2)}) %collective-permute-start) | collective-permute-done | bytes 262176 | tf_op jit(solution)/shard_map/ppermute | solution.py:235
  18.3 5.6 %collective-permute-done.1.kf = bf16[256,512]{1,0:T(8,128)(2,1)S(1)} collective-permute-done((bf16[256,512]{1,0:T(8,128)(2,1)S(1)}, bf16[256,512]{1,0:T(8,128)(2,1)S(1)}, u32[]{:S(2)}, u32[]{:S(2)}) %collective-permute-start.1) | collective-permute-done | bytes 262176 | tf_op jit(solution)/shard_map/ppermute | solution.py:235
  23.9 4.8 %collective-permute-done.2.vf = bf16[256,512]{1,0:T(8,128)(2,1)S(1)} collective-permute-done((bf16[256,512]{1,0:T(8,128)(2,1)S(1)}, bf16[256,512]{1,0:T(8,128)(2,1)S(1)}, u32[]{:S(2)}, u32[]{:S(2)}) %collective-permute-start.2) | collective-permute-done | bytes 262176 | tf_op jit(solution)/shard_map/ppermute | solution.py:235
  28.7 1.0 copy-done
  30.8 1.0 copy-done.4
  31.9 5.0 %shard_map.101.att = bf16[512,512]{1,0:T(8,128)(2,1)} custom-call(s32[1]{0:T(128)} %bitcast.me, s32[512,1]{1,0:T(8,128)S(1)} %copy.29.rid, s32[1,512]{1,0:T(1,128)S(1)} %bitcast.71, bf16[256,1024]{1,0:T(8,128)(2,1)S(1)} %copy-done, bf16[256,512]{1,0:T(8,128)(2,1)S(1)} %collective-permute-done.qf, bf16[256,1024]{1,0:T(8,128)(2,1)S(1)} %copy-done.2, ...), custom_call_target="tpu_custom_call" | custom-call | flops 2147483648 | bytes 2097152 | tf_op jit(solution)/shard_map/pallas_call | solution.py:207
  36.9 1.8 %collective-permute-start.5 = (bf16[256,1536]{1,0:T(8,128)(2,1)S(1)}, bf16[256,1536]{1,0:T(8,128)(2,1)}, u32[]{:S(2)}, u32[]{:S(2)}) collective-permute-start(bf16[256,1536]{1,0:T(8,128)(2,1)S(1)} %copy-done.10), channel_id=1, source_target_pairs={{0,16},{16,0},{1,17},{17,1},{2,18},{18,2},{3,19},{19,3},{4,20},{20... | collective-permute-start | bytes 2359304 | tf_op jit(solution)/shard_map/ppermute | solution.py:235
  38.7 3.3 %constant_dynamic-slice_fusion.1 = (bf16[2,1,512,1536]{3,2,1,0:T(8,128)(2,1)S(1)}, bf16[2,1,512,1536]{3,2,1,0:T(8,128)(2,1)S(1)}) fusion(bf16[2,2,512,1536]{3,2,1,0:T(8,128)(2,1)} %bitcast.74, s32[]{:T(128)S(6)} %select_n.100, s32[]{:T(128)S(6)} %select_n.101), kind=kLoop, calls=%fused_computation.54 | loop fusion | bytes 12582920 | tf_op jit(solution)/shard_map/jit(dynamic_index_in_dim)/dynamic_slice | solution.py:249
  42.0 1.8 %fusion.13 = bf16[256,1024]{1,0:T(8,128)(2,1)} fusion(bf16[1024,1536]{1,0:T(8,128)(2,1)S(1)} %bitcast.81, bf16[256,1536]{1,0:T(8,128)(2,1)S(1)} %copy-done.10), kind=kOutput, calls=%fused_computation.23 | convolution fusion | flops 805568512 | bytes 4456448 | tf_op jit(solution)/shard_map/dot_general | solution.py:226
  44.1 13.5 %collective-permute-done.5 = bf16[256,1536]{1,0:T(8,128)(2,1)} collective-permute-done((bf16[256,1536]{1,0:T(8,128)(2,1)S(1)}, bf16[256,1536]{1,0:T(8,128)(2,1)}, u32[]{:S(2)}, u32[]{:S(2)}) %collective-permute-start.5) | collective-permute-done | bytes 786464 | tf_op jit(solution)/shard_map/ppermute | solution.py:235
  57.6 2.9 %fusion.12 = bf16[256,1024]{1,0:T(8,128)(2,1)} fusion(bf16[1024,1536]{1,0:T(8,128)(2,1)S(1)} %bitcast.82, bf16[256,1536]{1,0:T(8,128)(2,1)} %collective-permute-done.5), kind=kOutput, calls=%fused_computation.22 | convolution fusion | flops 805568512 | bytes 4456448 | tf_op jit(solution)/shard_map/dot_general | solution.py:226
  60.5 1.7 %collective-permute-start.6 = (bf16[256,1024]{1,0:T(8,128)(2,1)}, bf16[256,1024]{1,0:T(8,128)(2,1)S(1)}, u32[]{:S(2)}, u32[]{:S(2)}) collective-permute-start(bf16[256,1024]{1,0:T(8,128)(2,1)} %fusion.12), channel_id=1, source_target_pairs={{0,16},{16,0},{1,17},{17,1},{2,18},{18,2},{3,19},{19,3},{4,20},{20... | collective-permute-start | bytes 1572872 | tf_op jit(solution)/shard_map/ppermute | solution.py:235
  63.3 3.1 %fusion.11 = bf16[256,1024]{1,0:T(8,128)(2,1)S(1)} fusion(bf16[1024,1536]{1,0:T(8,128)(2,1)} %bitcast.80, bf16[256,1536]{1,0:T(8,128)(2,1)} %collective-permute-done.5), kind=kOutput, calls=%fused_computation.21 | convolution fusion | flops 805568512 | bytes 4456448 | tf_op jit(solution)/shard_map/dot_general | solution.py:226
  66.4 11.8 %collective-permute-done.6 = bf16[256,1024]{1,0:T(8,128)(2,1)S(1)} collective-permute-done((bf16[256,1024]{1,0:T(8,128)(2,1)}, bf16[256,1024]{1,0:T(8,128)(2,1)S(1)}, u32[]{:S(2)}, u32[]{:S(2)}) %collective-permute-start.6) | collective-permute-done | bytes 524320 | tf_op jit(solution)/shard_map/ppermute | solution.py:235
  79.0 1.5 pad_maximum_fusion
  80.6 3.9 %all-gather.3.cloned.1.call-done = bf16[2048,512]{1,0:T(8,128)(2,1)} async-done(((bf16[512,512]{1,0:T(8,128)(2,1)}), bf16[2048,512]{1,0:T(8,128)(2,1)}) %all-gather.3.cloned.1.call-update) | async-done | bytes 2097168 | tf_op jit(solution)/shard_map/all_gather | solution.py:270
  84.5 1.3 constant_dynamic-slice_fusion.2
  85.8 1.5 collective-permute-start.3
  87.3 23.4 %collective-permute-done.3 = bf16[2,512,512]{2,1,0:T(8,128)(2,1)S(1)} collective-permute-done((bf16[2,512,512]{2,1,0:T(8,128)(2,1)S(1)}, bf16[2,512,512]{2,1,0:T(8,128)(2,1)S(1)}, u32[]{:S(2)}, u32[]{:S(2)}) %collective-permute-start.3) | collective-permute-done | bytes 1048608 | tf_op jit(solution)/shard_map/ppermute | solution.py:235
  110.7 1.7 %select_bitcast_fusion.3 = (bf16[2,1,256,512]{3,2,1,0:T(8,128)(2,1)S(1)}, bf16[2,1,256,512]{3,2,1,0:T(8,128)(2,1)S(1)}, bf16[2,1,256,512]{3,2,1,0:T(8,128)(2,1)S(1)}, bf16[2,1,256,512]{3,2,1,0:T(8,128)(2,1)S(1)}) fusion(pred[]{:T(512)S(6)} %eq.3, bf16[2,512,512]{2,1,0:T(8,128)(2,1)S(1)} %collective-permute-done.3, bf16[4,512,512]{2,1,0:T(8,128)(2,1)} %bitcast.84, ...), kind=kLoop, calls=%fused_computation.41 | loop fusion | flops 1048576 | bytes 4194313 | tf_op jit(solution)/shard_map/stack | solution.py:275
  112.4 5.7 %fusion = bf16[256,1536]{1,0:T(8,128)(2,1)} fusion(bf16[2,2,512,1536]{3,2,1,0:T(8,128)(2,1)} %bitcast.75, bf16[2,1,256,512]{3,2,1,0:T(8,128)(2,1)S(1)} %get-tuple-element.24, bf16[2,1,256,512]{3,2,1,0:T(8,128)(2,1)S(1)} %get-tuple-element.23), kind=kOutput, calls=%fused_computation.3 | convolution fusion | flops 1611530240 | bytes 8126464 | tf_op jit(solution)/shard_map/dot_general | solution.py:283
  118.1 1.5 collective-permute-start.4
  119.6 6.6 %convolution_convert_fusion = bf16[2,2,512,1536]{3,2,1,0:T(8,128)(2,1)} fusion(bf16[2,1,256,512]{3,2,1,0:T(8,128)(2,1)S(1)} %get-tuple-element.24, bf16[2,1,256,512]{3,2,1,0:T(8,128)(2,1)S(1)} %get-tuple-element.23, bf16[2,1,256,512]{3,2,1,0:T(8,128)(2,1)S(1)} %get-tuple-element.22, bf16[2,1,256,512]{3,2,1,0:T(8,128)(2,1)S(1)} %get-tuple-element.21, ...), kind=kOutput, calls=%fused_computation | convolution fusion | flops 3235905536 | bytes 9961472 | tf_op jit(solution)/shard_map/dot_general | solution.py:291
  126.2 3.1 %reduce-scatter.2.cloned.1.call-done.datt = bf16[512,512]{1,0:T(8,128)(2,1)} async-done(((bf16[2048,512]{1,0:T(8,128)(2,1)}), bf16[512,512]{1,0:T(8,128)(2,1)}) %reduce-scatter.2.cloned.1.call-update) | async-done | bytes 524304 | tf_op jit(solution)/shard_map/reduce_scatter | solution.py:263
  130.4 7.4 %shard_map.102 = (bf16[256,512]{1,0:T(8,128)(2,1)S(1)}, bf16[256,512]{1,0:T(8,128)(2,1)S(1)}, bf16[256,512]{1,0:T(8,128)(2,1)S(1)}, bf16[256,512]{1,0:T(8,128)(2...) custom-call(s32[1]{0:T(128)} %bitcast.me, s32[512,1]{1,0:T(8,128)S(1)} %copy.29.rid, ...), custom_call_target="tpu_custom_call" | custom-call | flops 5368709120 | bytes 4718592 | tf_op jit(solution)/shard_map/pallas_call | solution.py:207
  137.8 1.5 collective-permute-start.8
  139.9 5.7 %add_convert_fusion = bf16[256,1536]{1,0:T(8,128)(2,1)} fusion(bf16[256,1536]{1,0:T(8,128)(2,1)} %collective-permute-done.4, bf16[2,2,512,1536]{3,2,1,0:T(8,128)(2,1)} %bitcast.76, bf16[2,1,256,512]{3,2,1,0:T(8,128)(2,1)S(1)} %copy-done.9, bf16[2,1,256,512]{3,2,1,0:T(8,128)(2,1)S(1)} %get-tuple-element.21), kind=kOutput, calls=%fused_computation.15 | convolution fusion | flops 1612316672 | bytes 8912896 | tf_op jit(solution)/shard_map/dot_general | solution.py:283
  145.6 1.5 collective-permute-start.10
  147.2 5.6 %collective-permute-done.9 = bf16[256,512]{1,0:T(8,128)(2,1)S(1)} collective-permute-done((bf16[256,512]{1,0:T(8,128)(2,1)S(1)}, bf16[256,512]{1,0:T(8,128)(2,1)S(1)}, u32[]{:S(2)}, u32[]{:S(2)}) %collective-permute-start.9) | collective-permute-done | bytes 262176 | tf_op jit(solution)/shard_map/ppermute | solution.py:235
  154.5 2.6 %collective-permute-done.10 = bf16[256,512]{1,0:T(8,128)(2,1)S(1)} collective-permute-done((bf16[256,512]{1,0:T(8,128)(2,1)S(1)}, bf16[256,512]{1,0:T(8,128)(2,1)S(1)}, u32[]{:S(2)}, u32[]{:S(2)}) %collective-permute-start.10) | collective-permute-done | bytes 262176 | tf_op jit(solution)/shard_map/ppermute | solution.py:235
  (52 shorter events, 11.7 us)
Async XLA Ops:
  7.2 77.3 %all-gather.3.cloned.1.call-start = ((), (), s32[]{:S(2)}) async-start(), calls=%async_computation.2 | async-start | bytes 2621440 | tf_op jit(solution)/shard_map/all_gather | solution.py:270
  8.2 10.1 %collective-permute-start = (bf16[256,512]{1,0:T(8,128)(2,1)S(1)}, bf16[256,512]{1,0:T(8,128)(2,1)S(1)}, u32[]{:S(2)}, u32[]{:S(2)}) collective-permute-start(bf16[256,512]{1,0:T(8,128)(2,1)S(1)} %constant_dynamic-slice_fusion.5), channel_id=1, source_target_pairs={{0,16},{16,0},{1,17},{17,1},{2,18},{18,2},{3,19},{19,3},{4,20},{20... | collective-permute-start | bytes 786440 | tf_op jit(solution)/shard_map/ppermute | solution.py:235
  12.2 11.8 %collective-permute-start.1 = (bf16[256,512]{1,0:T(8,128)(2,1)S(1)}, bf16[256,512]{1,0:T(8,128)(2,1)S(1)}, u32[]{:S(2)}, u32[]{:S(2)}) collective-permute-start(bf16[256,512]{1,0:T(8,128)(2,1)S(1)} %constant_dynamic-slice_fusion.4), channel_id=1, source_target_pairs={{0,16},{16,0},{1,17},{17,1},{2,18},{18,2},{3,19},{19,3},{4,20},{20... | collective-permute-start | bytes 786440 | tf_op jit(solution)/shard_map/ppermute | solution.py:235
  13.2 15.5 %collective-permute-start.2 = (bf16[256,512]{1,0:T(8,128)(2,1)S(1)}, bf16[256,512]{1,0:T(8,128)(2,1)S(1)}, u32[]{:S(2)}, u32[]{:S(2)}) collective-permute-start(bf16[256,512]{1,0:T(8,128)(2,1)S(1)} %constant_dynamic-slice_fusion.3), channel_id=1, source_target_pairs={{0,16},{16,0},{1,17},{17,1},{2,18},{18,2},{3,19},{19,3},{4,20},{20... | collective-permute-start | bytes 786440 | tf_op jit(solution)/shard_map/ppermute | solution.py:235
  28.7 1.0 copy-start
  29.8 1.0 copy-start.2
  30.8 1.0 copy-start.4
  31.9 5.1 %copy-start.10 = (bf16[256,1536]{1,0:T(8,128)(2,1)S(1)}, bf16[256,1536]{1,0:T(8,128)(2,1)}, u32[]{:S(2)}) copy-start(bf16[256,1536]{1,0:T(8,128)(2,1)} %param.11) | copy-start | bytes 2359300
  36.9 92.5 %reduce-scatter.2.cloned.1.call-start = ((), (), s32[]{:S(2)}) async-start(), calls=%async_computation.1 | async-start | bytes 2621440 | tf_op jit(solution)/shard_map/reduce_scatter | solution.py:263
  36.9 20.6 %collective-permute-start.5 = (bf16[256,1536]{1,0:T(8,128)(2,1)S(1)}, bf16[256,1536]{1,0:T(8,128)(2,1)}, u32[]{:S(2)}, u32[]{:S(2)}) collective-permute-start(bf16[256,1536]{1,0:T(8,128)(2,1)S(1)} %copy-done.10), channel_id=1, source_target_pairs={{0,16},{16,0},{1,17},{17,1},{2,18},{18,2},{3,19},{19,3},{4,20},{20... | collective-permute-start | bytes 2359304 | tf_op jit(solution)/shard_map/ppermute | solution.py:235
  42.0 20.3 %copy-start.7 = (bf16[2,1,512,1536]{3,2,1,0:T(8,128)(2,1)}, bf16[2,1,512,1536]{3,2,1,0:T(8,128)(2,1)S(1)}, u32[]{:S(2)}) copy-start(bf16[2,1,512,1536]{3,2,1,0:T(8,128)(2,1)S(1)} %get-tuple-element.19) | copy-start | bytes 9437188
  43.8 34.4 %collective-permute-start.7 = (bf16[256,1024]{1,0:T(8,128)(2,1)}, bf16[256,1024]{1,0:T(8,128)(2,1)S(1)}, u32[]{:S(2)}, u32[]{:S(2)}) collective-permute-start(bf16[256,1024]{1,0:T(8,128)(2,1)} %fusion.13), channel_id=1, source_target_pairs={{0,16},{16,0},{1,17},{17,1},{2,18},{18,2},{3,19},{19,3},{4,20},{20... | collective-permute-start | bytes 1572872 | tf_op jit(solution)/shard_map/ppermute | solution.py:235
  60.5 17.7 %collective-permute-start.6 = (bf16[256,1024]{1,0:T(8,128)(2,1)}, bf16[256,1024]{1,0:T(8,128)(2,1)S(1)}, u32[]{:S(2)}, u32[]{:S(2)}) collective-permute-start(bf16[256,1024]{1,0:T(8,128)(2,1)} %fusion.12), channel_id=1, source_target_pairs={{0,16},{16,0},{1,17},{17,1},{2,18},{18,2},{3,19},{19,3},{4,20},{20... | collective-permute-start | bytes 1572872 | tf_op jit(solution)/shard_map/ppermute | solution.py:235
  85.8 25.0 %collective-permute-start.3 = (bf16[2,512,512]{2,1,0:T(8,128)(2,1)S(1)}, bf16[2,512,512]{2,1,0:T(8,128)(2,1)S(1)}, u32[]{:S(2)}, u32[]{:S(2)}) collective-permute-start(bf16[2,512,512]{2,1,0:T(8,128)(2,1)S(1)} %constant_dynamic-slice_fusion.2), channel_id=1, source_target_pairs={{0,16},{16,0},{1,17},{17,1},{2,18},{18,2},{3,19},{19,3},{4,20},{20... | collective-permute-start | bytes 3145736 | tf_op jit(solution)/shard_map/ppermute | solution.py:235
  112.4 7.2 %copy-start.8 = (bf16[2,1,256,512]{3,2,1,0:T(8,128)(2,1)}, bf16[2,1,256,512]{3,2,1,0:T(8,128)(2,1)S(1)}, u32[]{:S(2)}) copy-start(bf16[2,1,256,512]{3,2,1,0:T(8,128)(2,1)S(1)} %get-tuple-element.22) | copy-start | bytes 1572868
  112.4 7.1 %copy-start.11 = (bf16[256,1536]{1,0:T(8,128)(2,1)S(1)}, bf16[256,1536]{1,0:T(8,128)(2,1)}, u32[]{:S(2)}) copy-start(bf16[256,1536]{1,0:T(8,128)(2,1)} %param.11) | copy-start | bytes 2359300
  118.1 21.8 %collective-permute-start.4 = (bf16[256,1536]{1,0:T(8,128)(2,1)}, bf16[256,1536]{1,0:T(8,128)(2,1)}, u32[]{:S(2)}, u32[]{:S(2)}) collective-permute-start(bf16[256,1536]{1,0:T(8,128)(2,1)} %fusion), channel_id=1, source_target_pairs={{0,16},{16,0},{1,17},{17,1},{2,18},{18,2},{3,19},{19,3},{4,20},{20... | collective-permute-start | bytes 2359304 | tf_op jit(solution)/shard_map/ppermute | solution.py:235
  119.6 9.8 %copy-start.1 = (bf16[256,1024]{1,0:T(8,128)(2,1)S(1)}, bf16[256,1024]{1,0:T(8,128)(2,1)}, u32[]{:S(2)}) copy-start(bf16[256,1024]{1,0:T(8,128)(2,1)} %qo.3) | copy-start | bytes 1572868
  119.6 9.8 %copy-start.3 = (bf16[256,1024]{1,0:T(8,128)(2,1)S(1)}, bf16[256,1024]{1,0:T(8,128)(2,1)}, u32[]{:S(2)}) copy-start(bf16[256,1024]{1,0:T(8,128)(2,1)} %ko.3) | copy-start | bytes 1572868
  119.6 9.8 %copy-start.5 = (bf16[256,1024]{1,0:T(8,128)(2,1)S(1)}, bf16[256,1024]{1,0:T(8,128)(2,1)}, u32[]{:S(2)}) copy-start(bf16[256,1024]{1,0:T(8,128)(2,1)} %vo.3) | copy-start | bytes 1572868
  129.4 1.0 copy-start.6
  130.4 9.5 %copy-start.9 = (bf16[2,1,256,512]{3,2,1,0:T(8,128)(2,1)S(1)}, bf16[2,1,256,512]{3,2,1,0:T(8,128)(2,1)}, u32[]{:S(2)}) copy-start(bf16[2,1,256,512]{3,2,1,0:T(8,128)(2,1)} %copy-done.8) | copy-start | bytes 1572868
  137.8 9.3 %collective-permute-start.8 = (bf16[256,512]{1,0:T(8,128)(2,1)S(1)}, bf16[256,512]{1,0:T(8,128)(2,1)S(1)}, u32[]{:S(2)}, u32[]{:S(2)}) collective-permute-start(bf16[256,512]{1,0:T(8,128)(2,1)S(1)} %get-tuple-element.12), channel_id=1, source_target_pairs={{0,16},{16,0},{1,17},{17,1},{2,18},{18,2},{3,19},{19,3},{4,20},{20... | collective-permute-start | bytes 786440 | tf_op jit(solution)/shard_map/ppermute | solution.py:235
  139.4 13.4 %collective-permute-start.9 = (bf16[256,512]{1,0:T(8,128)(2,1)S(1)}, bf16[256,512]{1,0:T(8,128)(2,1)S(1)}, u32[]{:S(2)}, u32[]{:S(2)}) collective-permute-start(bf16[256,512]{1,0:T(8,128)(2,1)S(1)} %get-tuple-element.14), channel_id=1, source_target_pairs={{0,16},{16,0},{1,17},{17,1},{2,18},{18,2},{3,19},{19,3},{4,20},{20... | collective-permute-start | bytes 786440 | tf_op jit(solution)/shard_map/ppermute | solution.py:235
  145.6 11.4 %collective-permute-start.10 = (bf16[256,512]{1,0:T(8,128)(2,1)S(1)}, bf16[256,512]{1,0:T(8,128)(2,1)S(1)}, u32[]{:S(2)}, u32[]{:S(2)}) collective-permute-start(bf16[256,512]{1,0:T(8,128)(2,1)S(1)} %get-tuple-element.16), channel_id=1, source_target_pairs={{0,16},{16,0},{1,17},{17,1},{2,18},{18,2},{3,19},{19,3},{4,20},{20... | collective-permute-start | bytes 786440 | tf_op jit(solution)/shard_map/ppermute | solution.py:235
Sparse Core Ops, SparseCore 0:
  37.0 47.4 all-gather.2
  86.8 42.5 reduce-scatter.1

commit v2 on v1

--- a/solution.py
+++ b/solution.py
@@ -146,21 +146,23 @@
     same = row_ids == col_ids
     score = jnp.where(same, score, NEG)
     top = jnp.max(score, axis=1, keepdims=True)
-    weights = jnp.where(same, jnp.exp(score - top), 0.0)
+    weights = jnp.exp(score - top)
     return weights, jnp.sum(weights, axis=1, keepdims=True)
 
 
 def joined(own, far):
-    return jnp.concatenate([own[...], far[...]], axis=0)
-
-
-def forward_kernel(me, rid, cid, qo, qf, ko, kf, vo, vf, out):
+    return jnp.concatenate([own[...], far], axis=0)
+
+
+def forward_kernel(me, rid, cid, qo, ko, vo, far, out):
+    qf, kf, vf = far[0], far[1], far[2]
     weights, total = masked_softmax(joined(qo, qf), joined(ko, kf), rid[...], cid[...])
     acc = jnp.dot(weights.astype(jnp.bfloat16), joined(vo, vf), preferred_element_type=jnp.float32)
     out[...] = (acc / total).astype(jnp.bfloat16)
 
 
-def backward_kernel(me, rid, cid, qo, qf, ko, kf, vo, vf, att, datt, *outs):
+def backward_kernel(me, rid, cid, qo, ko, vo, far, att, datt, own_out, far_out):
+    qf, kf, vf = far[0], far[1], far[2]
     q, k, v = joined(qo, qf), joined(ko, kf), joined(vo, vf)
     d_out = datt[...]
     weights, total = masked_softmax(q, k, rid[...], cid[...])
@@ -180,25 +182,24 @@
         d_score, q, (((0,), (0,)), ((), ())), preferred_element_type=jnp.float32
     ) * scale
     rows = qo.shape[0]
-    for grad, own, far in ((d_q, 0, 1), (d_k, 2, 3), (d_v, 4, 5)):
-        outs[own][...] = grad[:rows].astype(jnp.bfloat16)
-        outs[far][...] = grad[rows:].astype(jnp.bfloat16)
-
-
-def attention_call(kernel, me, ids, pairs, extra, split_out):
-    rows = pairs[0][1].shape[0]
-    width = pairs[0][1].shape[1]
+    for i, grad in enumerate((d_q, d_k, d_v)):
+        own_out[i] = grad[:rows].astype(jnp.bfloat16)
+        far_out[i] = grad[rows:].astype(jnp.bfloat16)
+
+
+def attention_call(kernel, me, ids, owns, fars, extra, split_out):
+    rows, width = fars.shape[1:]
     heads = width // HEAD_DIM
     own = pl.BlockSpec((rows, HEAD_DIM), lambda h, me: (0, me[0] * heads + h))
-    far = pl.BlockSpec((rows, HEAD_DIM), lambda h, me: (0, h))
+    far = pl.BlockSpec((3, rows, HEAD_DIM), lambda h, me: (0, 0, h))
     both = pl.BlockSpec((2 * rows, HEAD_DIM), lambda h, me: (0, h))
     whole = [
         pl.BlockSpec((2 * rows, 1), lambda h, me: (0, 0)),
         pl.BlockSpec((1, 2 * rows), lambda h, me: (0, 0)),
     ]
     if split_out:
-        out_specs = [far] * 6
-        out_shape = [jax.ShapeDtypeStruct((rows, width), jnp.bfloat16)] * 6
+        out_specs = [far] * 2
+        out_shape = [jax.ShapeDtypeStruct((3, rows, width), jnp.bfloat16)] * 2
     else:
         out_specs = both
         out_shape = jax.ShapeDtypeStruct((2 * rows, width), jnp.bfloat16)
@@ -209,17 +210,17 @@
         grid_spec=pltpu.PrefetchScalarGridSpec(
             num_scalar_prefetch=1,
             grid=(heads,),
-            in_specs=whole + [own, far] * 3 + [both] * len(extra),
+            in_specs=whole + [own] * 3 + [far] + [both] * len(extra),
             out_specs=out_specs,
         ),
         out_shape=out_shape,
         cost_estimate=pl.CostEstimate(
-            flops=cells * 2 * HEAD_DIM * matmuls * 4,
-            bytes_accessed=2 * rows * width * 2 * (4 + len(extra) + (3 if split_out else 0)),
-            transcendentals=cells,
+            flops=cells * 2 * HEAD_DIM * matmuls if split_out else 1000,
+            bytes_accessed=2 * rows * width * 2 * (4 + len(extra) + (3 if split_out else 0)) if split_out else 1000,
+            transcendentals=cells if split_out else 0,
         ),
         compiler_params=pltpu.CompilerParams(vmem_limit_bytes=48 << 20),
-    )(me, ids[:, None], ids[None, :], *[a for pair in pairs for a in pair], *extra)
+    )(me, ids[:, None], ids[None, :], *owns, fars, *extra)
 
 
 def dot_f32(a, b, left, right):
@@ -242,8 +243,9 @@
     def away(a):
         return lax.dynamic_slice_in_dim(a, (1 - me) * half, half, 1)
 
-    far_q, far_k, far_v = swap(away(query)), swap(away(key)), swap(away(value))
-    far_go = swap(grad_out)
+    fars = swap(jnp.stack([away(query), away(key), away(value)]))
+    fars, late_go = lax.optimization_barrier((fars, grad_out))
+    far_go = swap(late_go)
     features = out_weight.shape[1]
     weight = out_weight.reshape(side, 2, half, features)
     w_mine = lax.dynamic_index_in_dim(weight, me, 1, keepdims=False).reshape(side * half, features)
@@ -264,9 +266,9 @@
         parts.reshape(groups * 2 * rows, half), "mp", scatter_dimension=0, tiled=True
     )
 
-    pairs = ((query, far_q), (key, far_k), (value, far_v))
+    owns = (query, key, value)
     where_me = jnp.reshape(me, (1,)).astype(jnp.int32)
-    attention = attention_call(forward_kernel, where_me, ids, pairs, (), False)
+    attention = attention_call(forward_kernel, where_me, ids, owns, fars, (), False)
     every = lax.all_gather(attention, "mp", axis=0, tiled=False)
     mine = lax.dynamic_slice_in_dim(every, me * side, side, 0)
     theirs = swap(lax.dynamic_slice_in_dim(every, (1 - me) * side, side, 0))
@@ -279,13 +281,18 @@
     att_own = beside(mine_own, their_own)
     att_far = beside(mine_far, their_far)
 
-    def project(att):
+    def project(att, w):
         return lax.dot_general(
-            att, weight, (((0, 1, 3), (0, 1, 2)), ((), ())), preferred_element_type=jnp.float32
+            att,
+            w.reshape(side, half, features),
+            (((0, 2), (0, 1)), ((), ())),
+            preferred_element_type=jnp.float32,
         )
 
-    other = swap(project(att_far).astype(bf))
-    mixed = (project(att_own) + other.astype(jnp.float32)).astype(bf)
+    far_part = project(mine_far, w_mine)
+    other = swap((far_part + project(their_far, w_away)).astype(bf))
+    mixed = project(mine_own, w_mine) + project(their_own, w_away)
+    mixed = (mixed + other.astype(jnp.float32)).astype(bf)
     att_all = jnp.concatenate([att_own, att_far], 2)
     go_all = jnp.concatenate([grad_out, far_go], 0)
     grad_weight = lax.dot_general(
@@ -293,16 +300,16 @@
     ).astype(bf).reshape(out_weight.shape)
 
     grads = attention_call(
-        backward_kernel, where_me, ids, pairs, (attention, d_attention), True
-    )
-
-    def home(own, far):
-        got = swap(far)
-        return jnp.concatenate([jnp.where(first, own, got), jnp.where(first, got, own)], 1)
-
-    grad_query = home(grads[0], grads[1])
-    grad_key = home(grads[2], grads[3])
-    grad_value = home(grads[4], grads[5])
+        backward_kernel, where_me, ids, owns, fars, (attention, d_attention), True
+    )
+
+    own_grads, got = grads[0], swap(grads[1])
+
+    def home(i):
+        own, far = own_grads[i], got[i]
+        return jnp.concatenate([jnp.where(first, own, far), jnp.where(first, far, own)], 1)
+
+    grad_query, grad_key, grad_value = home(0), home(1), home(2)
     return (mixed, grad_query, grad_key, grad_value, grad_weight)
 
 

time: 165 us -> 165 us (level)
  waiting for transfers between devices: 76.3 us -> 82.4 us
  starting transfers between devices: 15.6 us -> 11.4 us
  matrix products: 26.8 us -> 25 us
    reduce_scatter x1, waiting for transfers between devices: 3.14 us -> 10.1 us  [paired_body(): lax.psum_scatter(parts.reshape(groups * 2 * rows, half), 'mp', scatter_di...]
    ppermute x11 -> x7, starting transfers between devices: 15.5 us -> 11.3 us  [paired_body(): swap = lambda a: lax.ppermute(a, 'seq', [(0, 1), (1, 0)])]
    dynamic_slice x4 -> x1, local copies, waits for them, and re-layouts: 6.16 us -> 3.26 us  [paired_body(): lax.dynamic_index_in_dim(weight, 1 - me, 1, keepdims=False)]
    all_gather x1, waiting for transfers between devices: 3.88 us -> 1.72 us  [paired_body(): every = lax.all_gather(attention, 'mp', axis=0, tiled=False)]
    another operation x0 -> x2, local copies, waits for them, and re-layouts: none -> 2.15 us  [paired_body(): fars = swap(jnp.stack([away(query), away(key), away(value)]))]
    unnamed x25 -> x43, local copies, waits for them, and re-layouts: 4.24 us -> 2.2 us
    ppermute x11 -> x7, waiting for transfers between devices: 69.2 us -> 70.5 us  [paired_body(): swap = lambda a: lax.ppermute(a, 'seq', [(0, 1), (1, 0)])]
    dot_general x2 -> x4, matrix products: 11.4 us -> 11.3 us  [project(): lax.dot_general(att, w.reshape(side, half, features), (((0, 2), (0, 1)),...]
  transfers between devices with their start and end apart: 13 -> 9, of which waited for: 10 -> 7; matrix products, arithmetic and copies ran while one was open for 24% -> 23% of each run, Pallas kernels for 5% -> 4%
where the time goes in v2:
time: 165 us; the launch traced here: 164 us
  waiting for transfers between devices  82.4 us (50%)
  matrix products  25 us (15%)
  between operations  14.3 us (9%)
  Pallas kernels  11.7 us (7%)
  starting transfers between devices  11.4 us (7%)
  local copies, waits for them, and re-layouts  11.2 us (7%)
  other arithmetic  8.09 us (5%)
    ppermute x7, waiting for transfers between devices, paired_body(): swap = lambda a: lax.ppermute(a, 'seq', [(0, 1), (1, 0)])  70.5 us
    pallas_call x2, Pallas kernels, attention_call(): pl.pallas_call(kernel, grid_spec=pltpu.PrefetchScalarGridSpec(num_scalar_...  11.7 us
    ppermute x7, starting transfers between devices, paired_body(): swap = lambda a: lax.ppermute(a, 'seq', [(0, 1), (1, 0)])  11.3 us
    dot_general x4, matrix products, project(): lax.dot_general(att, w.reshape(side, half, features), (((0, 2), (0, 1)),...  11.3 us
    reduce_scatter x1, waiting for transfers between devices, paired_body(): lax.psum_scatter(parts.reshape(groups * 2 * rows, half), 'mp', scatter_di...  10.1 us
    dot_general x4, matrix products, dot_f32(): lax.dot_general(a, b, (((left,), (right,)), ((), ())), preferred_element_...  8.38 us
    dot_general x1, matrix products, paired_body(): lax.dot_general(att_all, go_all, (((2,), (0,)), ((), ())), preferred_elem...  5.4 us
  transfers between devices with their start and end apart: 9, of which 7 were waited for; matrix products, arithmetic and copies ran while one was open for 23% of the time, Pallas kernels for 4%

profile of v2, /device:TPU:0, one launch (start us, length us, event | category | flops | bytes accessed | tf_op | source)
XLA Modules:
  0.0 164.1 jit_solution(8934882426505534780)
XLA Ops:
  7.3 1.1 dynamic-slice_bitcast_fusion.2
  8.3 1.1 dynamic-slice_bitcast_fusion
  9.5 3.0 %collective-permute-start = (bf16[3,256,512]{2,1,0:T(8,128)(2,1)S(1)}, bf16[3,256,512]{2,1,0:T(8,128)(2,1)S(1)}, u32[]{:S(2)}, u32[]{:S(2)}) collective-permute-start(bf16[3,256,512]{2,1,0:T(8,128)(2,1)S(1)} %pad_maximum_fusion.2), channel_id=1, source_target_pairs={{0,16},{16,0},{1,17},{17,1},{2,18},{18,2},{3,19},{19,3},{4,20},{20... | collective-permute-start | bytes 2359304 | tf_op jit(solution)/shard_map/ppermute | solution.py:236
  13.0 17.1 %collective-permute-done.far = bf16[3,256,512]{2,1,0:T(8,128)(2,1)S(1)} collective-permute-done((bf16[3,256,512]{2,1,0:T(8,128)(2,1)S(1)}, bf16[3,256,512]{2,1,0:T(8,128)(2,1)S(1)}, u32[]{:S(2)}, u32[]{:S(2)}) %collective-permute-start) | collective-permute-done | bytes 786464 | tf_op jit(solution)/shard_map/ppermute | solution.py:236
  30.1 4.8 %shard_map.101.att = bf16[512,512]{1,0:T(8,128)(2,1)} custom-call(s32[1]{0:T(128)} %bitcast.me, s32[512,1]{1,0:T(8,128)S(1)} %copy.25.rid, s32[1,512]{1,0:T(1,128)S(1)} %bitcast.121, bf16[256,1024]{1,0:T(8,128)(2,1)S(1)} %copy-done, bf16[256,1024]{1,0:T(8,128)(2,1)S(1)} %copy-done.1, bf16[256,1024]{1,0:T(8,128)(2,1)S(1)} %copy-done.2, ...), custom_call_target="tpu_custom_call" | custom-call | flops 1000 | bytes 1000 | tf_op jit(solution)/shard_map/pallas_call | solution.py:208
  35.0 1.8 %collective-permute-start.3 = (bf16[256,1536]{1,0:T(8,128)(2,1)S(1)}, bf16[256,1536]{1,0:T(8,128)(2,1)S(1)}, u32[]{:S(2)}, u32[]{:S(2)}) collective-permute-start(bf16[256,1536]{1,0:T(8,128)(2,1)S(1)} %copy-done.15), channel_id=1, source_target_pairs={{0,16},{16,0},{1,17},{17,1},{2,18},{18,2},{3,19},{19,3},{4,20},{20... | collective-permute-start | bytes 2359304 | tf_op jit(solution)/shard_map/ppermute | solution.py:236
  36.8 3.3 %constant_dynamic-slice_fusion = (bf16[2,1,512,1536]{3,2,1,0:T(8,128)(2,1)S(1)}, bf16[2,1,512,1536]{3,2,1,0:T(8,128)(2,1)S(1)}) fusion(bf16[2,2,512,1536]{3,2,1,0:T(8,128)(2,1)} %bitcast.128, s32[]{:T(128)S(6)} %select_n.112, s32[]{:T(128)S(6)} %select_n.110), kind=kLoop, calls=%fused_computation.62 | loop fusion | bytes 12582920 | tf_op jit(solution)/shard_map/jit(dynamic_index_in_dim)/dynamic_slice | solution.py:252
  40.1 2.4 %fusion.39 = bf16[256,1024]{1,0:T(8,128)(2,1)} fusion(bf16[1024,1536]{1,0:T(8,128)(2,1)S(1)} %bitcast.123, bf16[256,1536]{1,0:T(8,128)(2,1)S(1)} %copy-done.15), kind=kOutput, calls=%fused_computation.29 | convolution fusion | flops 805568512 | bytes 4456448 | tf_op jit(solution)/shard_map/dot_general | solution.py:227
  42.8 12.8 %collective-permute-done.3 = bf16[256,1536]{1,0:T(8,128)(2,1)S(1)} collective-permute-done((bf16[256,1536]{1,0:T(8,128)(2,1)S(1)}, bf16[256,1536]{1,0:T(8,128)(2,1)S(1)}, u32[]{:S(2)}, u32[]{:S(2)}) %collective-permute-start.3) | collective-permute-done | bytes 786464 | tf_op jit(solution)/shard_map/ppermute | solution.py:236
  55.5 1.8 %convolution_convert_fusion.2 = bf16[256,1024]{1,0:T(8,128)(2,1)} fusion(bf16[256,1536]{1,0:T(8,128)(2,1)S(1)} %collective-permute-done.3, bf16[1024,1536]{1,0:T(8,128)(2,1)S(1)} %bitcast.124), kind=kOutput, calls=%fused_computation.25 | convolution fusion | flops 805568512 | bytes 4456448 | tf_op jit(solution)/shard_map/dot_general | solution.py:227
  57.3 1.7 %collective-permute-start.4 = (bf16[256,1024]{1,0:T(8,128)(2,1)}, bf16[256,1024]{1,0:T(8,128)(2,1)}, u32[]{:S(2)}, u32[]{:S(2)}) collective-permute-start(bf16[256,1024]{1,0:T(8,128)(2,1)} %convolution_convert_fusion.2), channel_id=1, source_target_pairs={{0,16},{16,0},{1,17},{17,1},{2,18},{18,2},{3,19},{19,3},{4,20},{20... | collective-permute-start | bytes 1572872 | tf_op jit(solution)/shard_map/ppermute | solution.py:236
  59.1 1.0 fusion.38
  60.1 3.2 %convolution_convert_fusion.3 = bf16[256,1024]{1,0:T(8,128)(2,1)S(1)} fusion(bf16[256,1536]{1,0:T(8,128)(2,1)} %copy-done.18, bf16[1024,1536]{1,0:T(8,128)(2,1)} %bitcast.126), kind=kOutput, calls=%fused_computation.26 | convolution fusion | flops 805568512 | bytes 4456448 | tf_op jit(solution)/shard_map/dot_general | solution.py:227
  63.3 13.1 %collective-permute-done.4 = bf16[256,1024]{1,0:T(8,128)(2,1)} collective-permute-done((bf16[256,1024]{1,0:T(8,128)(2,1)}, bf16[256,1024]{1,0:T(8,128)(2,1)}, u32[]{:S(2)}, u32[]{:S(2)}) %collective-permute-start.4) | collective-permute-done | bytes 524320 | tf_op jit(solution)/shard_map/ppermute | solution.py:236
  76.4 1.1 constant_dynamic-update-slice_fusion.1
  77.5 1.1 constant_dynamic-update-slice_fusion
  79.3 1.5 pad_maximum_fusion
  80.8 1.7 %all-gather.3.cloned.1.call-done = bf16[2048,512]{1,0:T(8,128)(2,1)} async-done(((bf16[512,512]{1,0:T(8,128)(2,1)}), bf16[2048,512]{1,0:T(8,128)(2,1)}) %all-gather.3.cloned.1.call-update) | async-done | bytes 2097168 | tf_op jit(solution)/shard_map/all_gather | solution.py:272
  82.5 2.3 %constant_dynamic-slice_fusion.1 = bf16[2,512,512]{2,1,0:T(8,128)(2,1)} fusion(bf16[4,512,512]{2,1,0:T(8,128)(2,1)} %bitcast.129, s32[]{:T(128)S(6)} %select_n.111), kind=kLoop, calls=%fused_computation.63 | loop fusion | bytes 2097156 | tf_op jit(solution)/shard_map/dynamic_slice | solution.py:274
  84.8 1.5 collective-permute-start.1
  86.3 4.4 %fusion.8 = f32[256,1536]{1,0:T(8,128)} fusion(bf16[2,1,512,1536]{3,2,1,0:T(8,128)(2,1)} %copy-done.7, bf16[4,512,512]{2,1,0:T(8,128)(2,1)} %bitcast.130, s32[]{:T(128)S(6)} %select_n.109), kind=kOutput, calls=%fused_computation.9 | convolution fusion | flops 805306368 | bytes 5242884 | tf_op jit(solution)/shard_map/dot_general | solution.py:285
  91.7 18.3 %collective-permute-done.1 = bf16[2,512,512]{2,1,0:T(8,128)(2,1)} collective-permute-done((bf16[2,512,512]{2,1,0:T(8,128)(2,1)}, bf16[2,512,512]{2,1,0:T(8,128)(2,1)}, u32[]{:S(2)}, u32[]{:S(2)}) %collective-permute-start.1) | collective-permute-done | bytes 1048608 | tf_op jit(solution)/shard_map/ppermute | solution.py:236
  110.0 2.9 %fusion.29 = bf16[256,1536]{1,0:T(8,128)(2,1)} fusion(f32[256,1536]{1,0:T(8,128)S(1)} %fusion.11, bf16[2,1,512,1536]{3,2,1,0:T(8,128)(2,1)S(1)} %copy-done.5, bf16[2,512,512]{2,1,0:T(8,128)(2,1)} %collective-permute-done.1), kind=kOutput, calls=%fused_computation.16 | convolution fusion | flops 806092800 | bytes 6029312 | tf_op jit(solution)/shard_map/dot_general | solution.py:285
  112.9 1.5 collective-permute-start.2
  114.4 2.9 %select_bitcast_fusion.3 = (bf16[2,1,256,512]{3,2,0,1:T(8,128)(2,1)}, bf16[2,1,256,512]{3,2,0,1:T(8,128)(2,1)}, bf16[2,1,256,512]{3,2,0,1:T(8,128)(2,1)}, bf16[2,1,256,512]{3,2,0,1:T(8,128)(2,1)}) fusion(pred[]{:T(512)S(6)} %eq.3, bf16[2,512,512]{2,1,0:T(8,128)(2,1)} %collective-permute-done.1, bf16[4,512,512]{2,1,0:T(8,128)(2,1)S(1)} %bitcast.132, ...), kind=kLoop, calls=%fused_computation.42 | loop fusion | flops 1048576 | bytes 4194313 | tf_op jit(solution)/shard_map/stack | solution.py:277
  117.3 10.1 %reduce-scatter.2.cloned.1.call-done.datt = bf16[512,512]{1,0:T(8,128)(2,1)} async-done(((bf16[2048,512]{1,0:T(8,128)(2,1)}), bf16[512,512]{1,0:T(8,128)(2,1)}) %reduce-scatter.2.cloned.1.call-update) | async-done | bytes 524304 | tf_op jit(solution)/shard_map/reduce_scatter | solution.py:265
  127.5 1.0 copy-done.3
  128.5 6.9 %shard_map.102 = (bf16[3,256,512]{2,1,0:T(8,128)(2,1)S(1)}, bf16[3,256,512]{2,1,0:T(8,128)(2,1)S(1)}) custom-call(s32[1]{0:T(128)} %bitcast.me, s32[512,1]{1,0:T(8,128)S(1)} %copy.25.rid, s32[1,512]{1,0:T(1,128)S(1)} %bitcast.122, bf16[256,1024]{1,0:T(8,128)(2,1)S(1)} %copy-done, bf16[256,1024]{1,0:T(8,128)(2,1)S(1)} %copy-done.1, ...), custom_call_target="tpu_custom_call" | custom-call | flops 1342177280 | bytes 4718592 | tf_op jit(solution)/shard_map/pallas_call | solution.py:208
  135.4 1.5 collective-permute-start.6
  137.0 5.4 %convolution_convert_fusion = bf16[2,2,512,1536]{3,2,1,0:T(8,128)(2,1)} fusion(bf16[256,1536]{1,0:T(8,128)(2,1)S(1)} %copy-done.19, bf16[256,1536]{1,0:T(8,128)(2,1)S(1)} %copy-done.17, bf16[2,1,256,512]{3,2,0,1:T(8,128)(2,1)S(1)} %copy-done.14, bf16[2,1,256,512]{3,2,0,1:T(8,128)(2,1)S(1)} %copy-done.13, bf16[2,1,256,512]{3,2,0,1:T(8,128)(2,1)S(1)} %copy-done.12, ...), kind=kOutput, calls=%fused_computation | convolution fusion | flops 3235905536 | bytes 9961472 | tf_op jit(solution)/shard_map/dot_general | solution.py:298
  142.4 3.0 %fusion.32 = bf16[256,1536]{1,0:T(8,128)(2,1)} fusion(f32[256,1536]{1,0:T(8,128)S(1)} %copy-done.9, bf16[2,1,512,1536]{3,2,1,0:T(8,128)(2,1)S(1)} %copy-done.6, bf16[256,1536]{1,0:T(8,128)(2,1)S(1)} %collective-permute-done.2, bf16[2,512,512]{2,1,0:T(8,128)(2,1)} %collective-permute-done.1), kind=kOutput, calls=%fused_computation.17 | convolution fusion | flops 806879232 | bytes 6815744 | tf_op jit(solution)/shard_map/dot_general | solution.py:285
  145.4 9.3 %collective-permute-done.6 = bf16[3,256,512]{2,1,0:T(8,128)(2,1)S(1)} collective-permute-done((bf16[3,256,512]{2,1,0:T(8,128)(2,1)S(1)}, bf16[3,256,512]{2,1,0:T(8,128)(2,1)S(1)}, u32[]{:S(2)}, u32[]{:S(2)}) %collective-permute-start.6) | collective-permute-done | bytes 786464 | tf_op jit(solution)/shard_map/ppermute | solution.py:236
  (62 shorter events, 5.4 us)
Async XLA Ops:
  7.2 22.9 %copy-start = (bf16[256,1024]{1,0:T(8,128)(2,1)S(1)}, bf16[256,1024]{1,0:T(8,128)(2,1)}, u32[]{:S(2)}) copy-start(bf16[256,1024]{1,0:T(8,128)(2,1)} %qo.3) | copy-start | bytes 1572868
  7.2 22.9 %copy-start.1 = (bf16[256,1024]{1,0:T(8,128)(2,1)S(1)}, bf16[256,1024]{1,0:T(8,128)(2,1)}, u32[]{:S(2)}) copy-start(bf16[256,1024]{1,0:T(8,128)(2,1)} %ko.3) | copy-start | bytes 1572868
  7.2 22.9 %copy-start.2 = (bf16[256,1024]{1,0:T(8,128)(2,1)S(1)}, bf16[256,1024]{1,0:T(8,128)(2,1)}, u32[]{:S(2)}) copy-start(bf16[256,1024]{1,0:T(8,128)(2,1)} %vo.3) | copy-start | bytes 1572868
  7.2 5.3 %copy-start.20 = (s32[12]{0:T(128)S(1)}, s32[12]{0:T(128)}, u32[]{:S(2)}) copy-start(s32[12]{0:T(128)} %param.10) | copy-start | bytes 148
  7.2 75.3 %all-gather.3.cloned.1.call-start = ((), (), s32[]{:S(2)}) async-start(), calls=%async_computation.2 | async-start | bytes 2621440 | tf_op jit(solution)/shard_map/all_gather | solution.py:272
  9.5 20.5 %collective-permute-start = (bf16[3,256,512]{2,1,0:T(8,128)(2,1)S(1)}, bf16[3,256,512]{2,1,0:T(8,128)(2,1)S(1)}, u32[]{:S(2)}, u32[]{:S(2)}) collective-permute-start(bf16[3,256,512]{2,1,0:T(8,128)(2,1)S(1)} %pad_maximum_fusion.2), channel_id=1, source_target_pairs={{0,16},{16,0},{1,17},{17,1},{2,18},{18,2},{3,19},{19,3},{4,20},{20... | collective-permute-start | bytes 2359304 | tf_op jit(solution)/shard_map/ppermute | solution.py:236
  30.1 4.9 %copy-start.15 = (bf16[256,1536]{1,0:T(8,128)(2,1)S(1)}, bf16[256,1536]{1,0:T(8,128)(2,1)}, u32[]{:S(2)}) copy-start(bf16[256,1536]{1,0:T(8,128)(2,1)} %param.11) | copy-start | bytes 2359300
  34.9 92.5 %reduce-scatter.2.cloned.1.call-start = ((), (), s32[]{:S(2)}) async-start(), calls=%async_computation.1 | async-start | bytes 2621440 | tf_op jit(solution)/shard_map/reduce_scatter | solution.py:265
  35.0 20.5 %collective-permute-start.3 = (bf16[256,1536]{1,0:T(8,128)(2,1)S(1)}, bf16[256,1536]{1,0:T(8,128)(2,1)S(1)}, u32[]{:S(2)}, u32[]{:S(2)}) collective-permute-start(bf16[256,1536]{1,0:T(8,128)(2,1)S(1)} %copy-done.15), channel_id=1, source_target_pairs={{0,16},{16,0},{1,17},{17,1},{2,18},{18,2},{3,19},{19,3},{4,20},{20... | collective-permute-start | bytes 2359304 | tf_op jit(solution)/shard_map/ppermute | solution.py:236
  40.1 15.5 %copy-start.4 = (bf16[2,1,512,1536]{3,2,1,0:T(8,128)(2,1)}, bf16[2,1,512,1536]{3,2,1,0:T(8,128)(2,1)S(1)}, u32[]{:S(2)}) copy-start(bf16[2,1,512,1536]{3,2,1,0:T(8,128)(2,1)S(1)} %get-tuple-element.15) | copy-start | bytes 9437188
  40.1 19.0 %copy-start.7 = (bf16[2,1,512,1536]{3,2,1,0:T(8,128)(2,1)}, bf16[2,1,512,1536]{3,2,1,0:T(8,128)(2,1)S(1)}, u32[]{:S(2)}) copy-start(bf16[2,1,512,1536]{3,2,1,0:T(8,128)(2,1)S(1)} %get-tuple-element.16) | copy-start | bytes 9437188
  42.5 16.6 %copy-start.16 = (bf16[256,1536]{1,0:T(8,128)(2,1)S(1)}, bf16[256,1536]{1,0:T(8,128)(2,1)}, u32[]{:S(2)}) copy-start(bf16[256,1536]{1,0:T(8,128)(2,1)} %param.11) | copy-start | bytes 2359300
  42.5 35.0 %collective-permute-start.5 = (bf16[256,1024]{1,0:T(8,128)(2,1)}, bf16[256,1024]{1,0:T(8,128)(2,1)}, u32[]{:S(2)}, u32[]{:S(2)}) collective-permute-start(bf16[256,1024]{1,0:T(8,128)(2,1)} %fusion.39), channel_id=1, source_target_pairs={{0,16},{16,0},{1,17},{17,1},{2,18},{18,2},{3,19},{19,3},{4,20},{20... | collective-permute-start | bytes 1572872 | tf_op jit(solution)/shard_map/ppermute | solution.py:236
  55.5 3.5 %copy-start.18 = (bf16[256,1536]{1,0:T(8,128)(2,1)}, bf16[256,1536]{1,0:T(8,128)(2,1)S(1)}, u32[]{:S(2)}) copy-start(bf16[256,1536]{1,0:T(8,128)(2,1)S(1)} %collective-permute-done.3) | copy-start | bytes 2359300
  57.3 19.0 %collective-permute-start.4 = (bf16[256,1024]{1,0:T(8,128)(2,1)}, bf16[256,1024]{1,0:T(8,128)(2,1)}, u32[]{:S(2)}, u32[]{:S(2)}) collective-permute-start(bf16[256,1024]{1,0:T(8,128)(2,1)} %convolution_convert_fusion.2), channel_id=1, source_target_pairs={{0,16},{16,0},{1,17},{17,1},{2,18},{18,2},{3,19},{19,3},{4,20},{20... | collective-permute-start | bytes 1572872 | tf_op jit(solution)/shard_map/ppermute | solution.py:236
  84.8 25.2 %collective-permute-start.1 = (bf16[2,512,512]{2,1,0:T(8,128)(2,1)}, bf16[2,512,512]{2,1,0:T(8,128)(2,1)}, u32[]{:S(2)}, u32[]{:S(2)}) collective-permute-start(bf16[2,512,512]{2,1,0:T(8,128)(2,1)} %constant_dynamic-slice_fusion.1), channel_id=1, source_target_pairs={{0,16},{16,0},{1,17},{17,1},{2,18},{18,2},{3,19},{19,3},{4,20},{20... | collective-permute-start | bytes 3145736 | tf_op jit(solution)/shard_map/ppermute | solution.py:236
  86.3 4.4 %copy-start.8 = (bf16[2,1,512,1536]{3,2,1,0:T(8,128)(2,1)S(1)}, bf16[2,1,512,1536]{3,2,1,0:T(8,128)(2,1)}, u32[]{:S(2)}) copy-start(bf16[2,1,512,1536]{3,2,1,0:T(8,128)(2,1)} %copy-done.7) | copy-start | bytes 9437188
  86.3 4.4 %copy-start.10 = (bf16[2048,512]{1,0:T(8,128)(2,1)S(1)}, bf16[2048,512]{1,0:T(8,128)(2,1)}, u32[]{:S(2)}) copy-start(bf16[2048,512]{1,0:T(8,128)(2,1)} %all-gather.3.cloned.1.call-done) | copy-start | bytes 6291460
  90.7 19.3 %copy-start.5 = (bf16[2,1,512,1536]{3,2,1,0:T(8,128)(2,1)S(1)}, bf16[2,1,512,1536]{3,2,1,0:T(8,128)(2,1)}, u32[]{:S(2)}) copy-start(bf16[2,1,512,1536]{3,2,1,0:T(8,128)(2,1)} %copy-done.4) | copy-start | bytes 9437188
  112.9 29.4 %collective-permute-start.2 = (bf16[256,1536]{1,0:T(8,128)(2,1)}, bf16[256,1536]{1,0:T(8,128)(2,1)S(1)}, u32[]{:S(2)}, u32[]{:S(2)}) collective-permute-start(bf16[256,1536]{1,0:T(8,128)(2,1)} %fusion.29), channel_id=1, source_target_pairs={{0,16},{16,0},{1,17},{17,1},{2,18},{18,2},{3,19},{19,3},{4,20},{20... | collective-permute-start | bytes 2359304 | tf_op jit(solution)/shard_map/ppermute | solution.py:236
  127.5 1.0 copy-start.3
  128.5 8.4 %copy-start.11 = (bf16[2,1,256,512]{3,2,0,1:T(8,128)(2,1)S(1)}, bf16[2,1,256,512]{3,2,0,1:T(8,128)(2,1)}, u32[]{:S(2)}) copy-start(bf16[2,1,256,512]{3,2,0,1:T(8,128)(2,1)} %get-tuple-element.17) | copy-start | bytes 1572868
  128.5 8.4 %copy-start.12 = (bf16[2,1,256,512]{3,2,0,1:T(8,128)(2,1)S(1)}, bf16[2,1,256,512]{3,2,0,1:T(8,128)(2,1)}, u32[]{:S(2)}) copy-start(bf16[2,1,256,512]{3,2,0,1:T(8,128)(2,1)} %get-tuple-element.18) | copy-start | bytes 1572868
  128.5 8.4 %copy-start.13 = (bf16[2,1,256,512]{3,2,0,1:T(8,128)(2,1)S(1)}, bf16[2,1,256,512]{3,2,0,1:T(8,128)(2,1)}, u32[]{:S(2)}) copy-start(bf16[2,1,256,512]{3,2,0,1:T(8,128)(2,1)} %get-tuple-element.19) | copy-start | bytes 1572868
  128.5 8.4 %copy-start.14 = (bf16[2,1,256,512]{3,2,0,1:T(8,128)(2,1)S(1)}, bf16[2,1,256,512]{3,2,0,1:T(8,128)(2,1)}, u32[]{:S(2)}) copy-start(bf16[2,1,256,512]{3,2,0,1:T(8,128)(2,1)} %get-tuple-element.20) | copy-start | bytes 1572868
  128.5 8.4 %copy-start.17 = (bf16[256,1536]{1,0:T(8,128)(2,1)S(1)}, bf16[256,1536]{1,0:T(8,128)(2,1)}, u32[]{:S(2)}) copy-start(bf16[256,1536]{1,0:T(8,128)(2,1)} %param.11) | copy-start | bytes 2359300
  128.5 8.4 %copy-start.19 = (bf16[256,1536]{1,0:T(8,128)(2,1)S(1)}, bf16[256,1536]{1,0:T(8,128)(2,1)}, u32[]{:S(2)}) copy-start(bf16[256,1536]{1,0:T(8,128)(2,1)} %copy-done.18) | copy-start | bytes 2359300
  135.4 19.2 %collective-permute-start.6 = (bf16[3,256,512]{2,1,0:T(8,128)(2,1)S(1)}, bf16[3,256,512]{2,1,0:T(8,128)(2,1)S(1)}, u32[]{:S(2)}, u32[]{:S(2)}) collective-permute-start(bf16[3,256,512]{2,1,0:T(8,128)(2,1)S(1)} %get-tuple-element.12), channel_id=1, source_target_pairs={{0,16},{16,0},{1,17},{17,1},{2,18},{18,2},{3,19},{19,3},{4,20},{20... | collective-permute-start | bytes 2359304 | tf_op jit(solution)/shard_map/ppermute | solution.py:236
  137.0 5.4 %copy-start.6 = (bf16[2,1,512,1536]{3,2,1,0:T(8,128)(2,1)S(1)}, bf16[2,1,512,1536]{3,2,1,0:T(8,128)(2,1)}, u32[]{:S(2)}) copy-start(bf16[2,1,512,1536]{3,2,1,0:T(8,128)(2,1)} %copy-done.4) | copy-start | bytes 9437188
  137.0 5.4 %copy-start.9 = (f32[256,1536]{1,0:T(8,128)S(1)}, f32[256,1536]{1,0:T(8,128)}, u32[]{:S(2)}) copy-start(f32[256,1536]{1,0:T(8,128)} %fusion.8) | copy-start | bytes 4718596
Sparse Core Ops, SparseCore 0:
  35.1 47.4 all-gather.2
  84.8 42.5 reduce-scatter.1

commit v3 on v2

--- a/solution.py
+++ b/solution.py
@@ -161,12 +161,43 @@
     out[...] = (acc / total).astype(jnp.bfloat16)
 
 
-def backward_kernel(me, rid, cid, qo, ko, vo, far, att, datt, own_out, far_out):
+def prob_kernel(me, rid, cid, qo, ko, far, out):
+    weights, total = masked_softmax(joined(qo, far[0]), joined(ko, far[1]), rid[...], cid[...])
+    out[0] = weights * (1.0 / total)
+
+
+def prob_call(me, ids, query, key, fars):
+    rows, width = fars.shape[1:]
+    heads = width // HEAD_DIM
+    own = pl.BlockSpec((rows, HEAD_DIM), lambda h, me: (0, me[0] * heads + h))
+    cells = 4 * rows * rows * heads
+    return pl.pallas_call(
+        prob_kernel,
+        grid_spec=pltpu.PrefetchScalarGridSpec(
+            num_scalar_prefetch=1,
+            grid=(heads,),
+            in_specs=[
+                pl.BlockSpec((2 * rows, 1), lambda h, me: (0, 0)),
+                pl.BlockSpec((1, 2 * rows), lambda h, me: (0, 0)),
+                own,
+                own,
+                pl.BlockSpec((3, rows, HEAD_DIM), lambda h, me: (0, 0, h)),
+            ],
+            out_specs=pl.BlockSpec((1, 2 * rows, 2 * rows), lambda h, me: (h, 0, 0)),
+        ),
+        out_shape=jax.ShapeDtypeStruct((heads, 2 * rows, 2 * rows), jnp.float32),
+        cost_estimate=pl.CostEstimate(
+            flops=cells * 2 * HEAD_DIM, bytes_accessed=cells * 4, transcendentals=cells
+        ),
+        compiler_params=pltpu.CompilerParams(vmem_limit_bytes=48 << 20),
+    )(me, ids[:, None], ids[None, :], query, key, fars)
+
+
+def backward_kernel(me, rid, cid, qo, ko, vo, far, att, datt, probs, own_out, far_out):
     qf, kf, vf = far[0], far[1], far[2]
     q, k, v = joined(qo, qf), joined(ko, kf), joined(vo, vf)
     d_out = datt[...]
-    weights, total = masked_softmax(q, k, rid[...], cid[...])
-    prob = weights * (1.0 / total)
+    prob = probs[0]
     delta = jnp.sum(
         d_out.astype(jnp.float32) * att[...].astype(jnp.float32), axis=1, keepdims=True
     )
@@ -193,6 +224,7 @@
     own = pl.BlockSpec((rows, HEAD_DIM), lambda h, me: (0, me[0] * heads + h))
     far = pl.BlockSpec((3, rows, HEAD_DIM), lambda h, me: (0, 0, h))
     both = pl.BlockSpec((2 * rows, HEAD_DIM), lambda h, me: (0, h))
+    square = pl.BlockSpec((1, 2 * rows, 2 * rows), lambda h, me: (h, 0, 0))
     whole = [
         pl.BlockSpec((2 * rows, 1), lambda h, me: (0, 0)),
         pl.BlockSpec((1, 2 * rows), lambda h, me: (0, 0)),
@@ -210,7 +242,7 @@
         grid_spec=pltpu.PrefetchScalarGridSpec(
             num_scalar_prefetch=1,
             grid=(heads,),
-            in_specs=whole + [own] * 3 + [far] + [both] * len(extra),
+            in_specs=whole + [own] * 3 + [far] + [both, both, square][: len(extra)],
             out_specs=out_specs,
         ),
         out_shape=out_shape,
@@ -299,8 +331,9 @@
         att_all, go_all, (((2,), (0,)), ((), ())), preferred_element_type=jnp.float32
     ).astype(bf).reshape(out_weight.shape)
 
+    probs = prob_call(where_me, ids, query, key, fars)
     grads = attention_call(
-        backward_kernel, where_me, ids, owns, fars, (attention, d_attention), True
+        backward_kernel, where_me, ids, owns, fars, (attention, d_attention, probs), True
     )
 
     own_grads, got = grads[0], swap(grads[1])

time: 165 us -> 163 us (0.988)
  Pallas kernels: 11.7 us -> 14.4 us
  matrix products: 25 us -> 22.7 us
  waiting for transfers between devices: 82.4 us -> 80.7 us
    pallas_call x0 -> x1, Pallas kernels: none -> 3.86 us  [prob_call(): pl.pallas_call(prob_kernel, grid_spec=pltpu.PrefetchScalarGridSpec(num_sc...]
    dot_general x4, matrix products: 11.3 us -> 8.99 us  [project(): lax.dot_general(att, w.reshape(side, half, features), (((0, 2), (0, 1)),...]
  transfers between devices with their start and end apart: 9 -> 9, of which waited for: 7 -> 7; matrix products, arithmetic and copies ran while one was open for 23% -> 22% of each run, Pallas kernels for 4% -> 6%
where the time goes in v3:
time: 163 us
  waiting for transfers between devices  80.7 us (50%)
  matrix products  22.7 us (14%)
  Pallas kernels  14.4 us (9%)
  between operations  14.3 us (9%)
  local copies, waits for them, and re-layouts  11.3 us (7%)
  starting transfers between devices  11.3 us (7%)
  other arithmetic  8.2 us (5%)
    ppermute x7, waiting for transfers between devices, paired_body(): swap = lambda a: lax.ppermute(a, 'seq', [(0, 1), (1, 0)])  69 us
    ppermute x7, starting transfers between devices, paired_body(): swap = lambda a: lax.ppermute(a, 'seq', [(0, 1), (1, 0)])  11.2 us
    pallas_call x2, Pallas kernels, attention_call(): pl.pallas_call(kernel, grid_spec=pltpu.PrefetchScalarGridSpec(num_scalar_...  10.5 us
    reduce_scatter x1, waiting for transfers between devices, paired_body(): lax.psum_scatter(parts.reshape(groups * 2 * rows, half), 'mp', scatter_di...  10 us
    dot_general x4, matrix products, project(): lax.dot_general(att, w.reshape(side, half, features), (((0, 2), (0, 1)),...  8.99 us
    dot_general x4, matrix products, dot_f32(): lax.dot_general(a, b, (((left,), (right,)), ((), ())), preferred_element_...  8.33 us
    dot_general x1, matrix products, paired_body(): lax.dot_general(att_all, go_all, (((2,), (0,)), ((), ())), preferred_elem...  5.4 us
    pallas_call x1, Pallas kernels, prob_call(): pl.pallas_call(prob_kernel, grid_spec=pltpu.PrefetchScalarGridSpec(num_sc...  3.86 us
  transfers between devices with their start and end apart: 9, of which 7 were waited for; matrix products, arithmetic and copies ran while one was open for 22% of the time, Pallas kernels for 6%

profile of v3, /device:TPU:0, one launch (start us, length us, event | category | flops | bytes accessed | tf_op | source)
XLA Modules:
  0.0 162.9 jit_solution(15469321016966433330)
XLA Ops:
  7.3 1.1 dynamic-slice_bitcast_fusion.2
  8.3 1.1 dynamic-slice_bitcast_fusion
  9.5 3.0 %collective-permute-start = (bf16[3,256,512]{2,1,0:T(8,128)(2,1)S(1)}, bf16[3,256,512]{2,1,0:T(8,128)(2,1)S(1)}, u32[]{:S(2)}, u32[]{:S(2)}) collective-permute-start(bf16[3,256,512]{2,1,0:T(8,128)(2,1)S(1)} %pad_maximum_fusion.2), channel_id=1, source_target_pairs={{0,16},{16,0},{1,17},{17,1},{2,18},{18,2},{3,19},{19,3},{4,20},{20... | collective-permute-start | bytes 2359304 | tf_op jit(solution)/shard_map/ppermute | solution.py:268
  13.0 17.1 %collective-permute-done.far = bf16[3,256,512]{2,1,0:T(8,128)(2,1)S(1)} collective-permute-done((bf16[3,256,512]{2,1,0:T(8,128)(2,1)S(1)}, bf16[3,256,512]{2,1,0:T(8,128)(2,1)S(1)}, u32[]{:S(2)}, u32[]{:S(2)}) %collective-permute-start) | collective-permute-done | bytes 786464 | tf_op jit(solution)/shard_map/ppermute | solution.py:268
  30.1 4.8 %shard_map.101.att = bf16[512,512]{1,0:T(8,128)(2,1)} custom-call(s32[1]{0:T(128)} %bitcast.me, s32[512,1]{1,0:T(8,128)S(1)} %copy.26.rid, s32[1,512]{1,0:T(1,128)S(1)} %bitcast.121, bf16[256,1024]{1,0:T(8,128)(2,1)S(1)} %copy-done, bf16[256,1024]{1,0:T(8,128)(2,1)S(1)} %copy-done.1, bf16[256,1024]{1,0:T(8,128)(2,1)S(1)} %copy-done.2, ...), custom_call_target="tpu_custom_call" | custom-call | flops 1000 | bytes 1000 | tf_op jit(solution)/shard_map/pallas_call | solution.py:240
  35.0 1.8 %collective-permute-start.3 = (bf16[256,1536]{1,0:T(8,128)(2,1)S(1)}, bf16[256,1536]{1,0:T(8,128)(2,1)S(1)}, u32[]{:S(2)}, u32[]{:S(2)}) collective-permute-start(bf16[256,1536]{1,0:T(8,128)(2,1)S(1)} %copy-done.15), channel_id=1, source_target_pairs={{0,16},{16,0},{1,17},{17,1},{2,18},{18,2},{3,19},{19,3},{4,20},{20... | collective-permute-start | bytes 2359304 | tf_op jit(solution)/shard_map/ppermute | solution.py:268
  36.8 3.3 %constant_dynamic-slice_fusion = (bf16[2,1,512,1536]{3,2,1,0:T(8,128)(2,1)S(1)}, bf16[2,1,512,1536]{3,2,1,0:T(8,128)(2,1)S(1)}) fusion(bf16[2,2,512,1536]{3,2,1,0:T(8,128)(2,1)} %bitcast.129, s32[]{:T(128)S(6)} %select_n.112, s32[]{:T(128)S(6)} %select_n.110), kind=kLoop, calls=%fused_computation.62 | loop fusion | bytes 12582920 | tf_op jit(solution)/shard_map/jit(dynamic_index_in_dim)/dynamic_slice | solution.py:284
  40.1 2.3 %fusion.39 = bf16[256,1024]{1,0:T(8,128)(2,1)} fusion(bf16[1024,1536]{1,0:T(8,128)(2,1)S(1)} %bitcast.124, bf16[256,1536]{1,0:T(8,128)(2,1)S(1)} %copy-done.15), kind=kOutput, calls=%fused_computation.29 | convolution fusion | flops 805568512 | bytes 4456448 | tf_op jit(solution)/shard_map/dot_general | solution.py:259
  42.7 12.8 %collective-permute-done.3 = bf16[256,1536]{1,0:T(8,128)(2,1)S(1)} collective-permute-done((bf16[256,1536]{1,0:T(8,128)(2,1)S(1)}, bf16[256,1536]{1,0:T(8,128)(2,1)S(1)}, u32[]{:S(2)}, u32[]{:S(2)}) %collective-permute-start.3) | collective-permute-done | bytes 786464 | tf_op jit(solution)/shard_map/ppermute | solution.py:268
  55.5 1.8 %convolution_convert_fusion.2 = bf16[256,1024]{1,0:T(8,128)(2,1)} fusion(bf16[256,1536]{1,0:T(8,128)(2,1)S(1)} %collective-permute-done.3, bf16[1024,1536]{1,0:T(8,128)(2,1)S(1)} %bitcast.125), kind=kOutput, calls=%fused_computation.25 | convolution fusion | flops 805568512 | bytes 4456448 | tf_op jit(solution)/shard_map/dot_general | solution.py:259
  57.3 1.7 %collective-permute-start.4 = (bf16[256,1024]{1,0:T(8,128)(2,1)}, bf16[256,1024]{1,0:T(8,128)(2,1)}, u32[]{:S(2)}, u32[]{:S(2)}) collective-permute-start(bf16[256,1024]{1,0:T(8,128)(2,1)} %convolution_convert_fusion.2), channel_id=1, source_target_pairs={{0,16},{16,0},{1,17},{17,1},{2,18},{18,2},{3,19},{19,3},{4,20},{20... | collective-permute-start | bytes 1572872 | tf_op jit(solution)/shard_map/ppermute | solution.py:268
  60.1 3.2 %convolution_convert_fusion.3 = bf16[256,1024]{1,0:T(8,128)(2,1)S(1)} fusion(bf16[256,1536]{1,0:T(8,128)(2,1)} %copy-done.18, bf16[1024,1536]{1,0:T(8,128)(2,1)} %bitcast.127), kind=kOutput, calls=%fused_computation.26 | convolution fusion | flops 805568512 | bytes 4456448 | tf_op jit(solution)/shard_map/dot_general | solution.py:259
  63.3 13.1 %collective-permute-done.4 = bf16[256,1024]{1,0:T(8,128)(2,1)} collective-permute-done((bf16[256,1024]{1,0:T(8,128)(2,1)}, bf16[256,1024]{1,0:T(8,128)(2,1)}, u32[]{:S(2)}, u32[]{:S(2)}) %collective-permute-start.4) | collective-permute-done | bytes 524320 | tf_op jit(solution)/shard_map/ppermute | solution.py:268
  76.4 1.1 constant_dynamic-update-slice_fusion.1
  77.5 1.1 constant_dynamic-update-slice_fusion
  79.3 1.6 pad_maximum_fusion
  80.9 1.7 %all-gather.3.cloned.1.call-done = bf16[2048,512]{1,0:T(8,128)(2,1)} async-done(((bf16[512,512]{1,0:T(8,128)(2,1)}), bf16[2048,512]{1,0:T(8,128)(2,1)}) %all-gather.3.cloned.1.call-update) | async-done | bytes 2097168 | tf_op jit(solution)/shard_map/all_gather | solution.py:304
  82.5 2.3 %constant_dynamic-slice_fusion.1 = bf16[2,512,512]{2,1,0:T(8,128)(2,1)} fusion(bf16[4,512,512]{2,1,0:T(8,128)(2,1)} %bitcast.130, s32[]{:T(128)S(6)} %select_n.111), kind=kLoop, calls=%fused_computation.63 | loop fusion | bytes 2097156 | tf_op jit(solution)/shard_map/dynamic_slice | solution.py:306
  84.8 1.5 collective-permute-start.1
  86.3 3.9 %shard_map.102.probs = f32[4,512,512]{2,1,0:T(8,128)} custom-call(s32[1]{0:T(128)} %bitcast.me, s32[512,1]{1,0:T(8,128)S(1)} %copy.26.rid, s32[1,512]{1,0:T(1,128)S(1)} %bitcast.122, bf16[256,1024]{1,0:T(8,128)(2,1)S(1)} %copy-done, bf16[256,1024]{1,0:T(8,128)(2,1)S(1)} %copy-done.1, bf16[3,256,512]{2,1,0:T(8,128)(2,1)S(1)} %collective-permute-done.far), custom_call_target="tpu_custom_call" | custom-call | flops 268435456 | bytes 4194304 | tf_op jit(solution)/shard_map/pallas_call | solution.py:174
  90.2 2.2 %fusion.8 = f32[256,1536]{1,0:T(8,128)} fusion(bf16[2,1,512,1536]{3,2,1,0:T(8,128)(2,1)S(1)} %copy-done.8, bf16[4,512,512]{2,1,0:T(8,128)(2,1)S(1)} %bitcast.131, s32[]{:T(128)S(6)} %select_n.109), kind=kOutput, calls=%fused_computation.9 | convolution fusion | flops 805306368 | bytes 5242884 | tf_op jit(solution)/shard_map/dot_general | solution.py:317
  93.3 16.7 %collective-permute-done.1 = bf16[2,512,512]{2,1,0:T(8,128)(2,1)} collective-permute-done((bf16[2,512,512]{2,1,0:T(8,128)(2,1)}, bf16[2,512,512]{2,1,0:T(8,128)(2,1)}, u32[]{:S(2)}, u32[]{:S(2)}) %collective-permute-start.1) | collective-permute-done | bytes 1048608 | tf_op jit(solution)/shard_map/ppermute | solution.py:268
  110.1 2.9 %fusion.29 = bf16[256,1536]{1,0:T(8,128)(2,1)} fusion(f32[256,1536]{1,0:T(8,128)S(1)} %fusion.11, bf16[2,1,512,1536]{3,2,1,0:T(8,128)(2,1)S(1)} %copy-done.5, bf16[2,512,512]{2,1,0:T(8,128)(2,1)} %collective-permute-done.1), kind=kOutput, calls=%fused_computation.16 | convolution fusion | flops 806092800 | bytes 6029312 | tf_op jit(solution)/shard_map/dot_general | solution.py:317
  113.0 1.5 collective-permute-start.2
  114.4 3.0 %select_bitcast_fusion.3 = (bf16[2,1,256,512]{3,2,0,1:T(8,128)(2,1)}, bf16[2,1,256,512]{3,2,0,1:T(8,128)(2,1)}, bf16[2,1,256,512]{3,2,0,1:T(8,128)(2,1)}, bf16[2,1,256,512]{3,2,0,1:T(8,128)(2,1)}) fusion(pred[]{:T(512)S(6)} %eq.3, bf16[2,512,512]{2,1,0:T(8,128)(2,1)} %collective-permute-done.1, bf16[4,512,512]{2,1,0:T(8,128)(2,1)S(1)} %bitcast.133, ...), kind=kLoop, calls=%fused_computation.42 | loop fusion | flops 1048576 | bytes 4194313 | tf_op jit(solution)/shard_map/stack | solution.py:309
  117.4 10.0 %reduce-scatter.2.cloned.1.call-done.datt = bf16[512,512]{1,0:T(8,128)(2,1)} async-done(((bf16[2048,512]{1,0:T(8,128)(2,1)}), bf16[512,512]{1,0:T(8,128)(2,1)}) %reduce-scatter.2.cloned.1.call-update) | async-done | bytes 524304 | tf_op jit(solution)/shard_map/reduce_scatter | solution.py:297
  127.5 1.0 copy-done.3
  128.6 5.7 %shard_map.103 = (bf16[3,256,512]{2,1,0:T(8,128)(2,1)S(1)}, bf16[3,256,512]{2,1,0:T(8,128)(2,1)S(1)}) custom-call(s32[1]{0:T(128)} %bitcast.me, s32[512,1]{1,0:T(8,128)S(1)} %copy.26.rid, s32[1,512]{1,0:T(1,128)S(1)} %bitcast.123, bf16[256,1024]{1,0:T(8,128)(2,1)S(1)} %copy-done, bf16[256,1024]{1,0:T(8,128)(2,1)S(1)} %copy-done.1, ...), custom_call_target="tpu_custom_call" | custom-call | flops 1342177280 | bytes 5242880 | tf_op jit(solution)/shard_map/pallas_call | solution.py:240
  134.2 1.5 collective-permute-start.6
  135.8 5.4 %convolution_convert_fusion = bf16[2,2,512,1536]{3,2,1,0:T(8,128)(2,1)} fusion(bf16[256,1536]{1,0:T(8,128)(2,1)S(1)} %copy-done.19, bf16[256,1536]{1,0:T(8,128)(2,1)S(1)} %copy-done.17, bf16[2,1,256,512]{3,2,0,1:T(8,128)(2,1)S(1)} %copy-done.14, bf16[2,1,256,512]{3,2,0,1:T(8,128)(2,1)S(1)} %copy-done.13, bf16[2,1,256,512]{3,2,0,1:T(8,128)(2,1)S(1)} %copy-done.12, ...), kind=kOutput, calls=%fused_computation | convolution fusion | flops 3235905536 | bytes 9961472 | tf_op jit(solution)/shard_map/dot_general | solution.py:330
  141.2 3.0 %fusion.32 = bf16[256,1536]{1,0:T(8,128)(2,1)} fusion(f32[256,1536]{1,0:T(8,128)S(1)} %copy-done.9, bf16[2,1,512,1536]{3,2,1,0:T(8,128)(2,1)S(1)} %copy-done.6, bf16[256,1536]{1,0:T(8,128)(2,1)S(1)} %collective-permute-done.2, bf16[2,512,512]{2,1,0:T(8,128)(2,1)} %collective-permute-done.1), kind=kOutput, calls=%fused_computation.17 | convolution fusion | flops 806879232 | bytes 6815744 | tf_op jit(solution)/shard_map/dot_general | solution.py:317
  144.1 9.3 %collective-permute-done.6 = bf16[3,256,512]{2,1,0:T(8,128)(2,1)S(1)} collective-permute-done((bf16[3,256,512]{2,1,0:T(8,128)(2,1)S(1)}, bf16[3,256,512]{2,1,0:T(8,128)(2,1)S(1)}, u32[]{:S(2)}, u32[]{:S(2)}) %collective-permute-start.6) | collective-permute-done | bytes 786464 | tf_op jit(solution)/shard_map/ppermute | solution.py:268
  (63 shorter events, 6.4 us)
Async XLA Ops:
  7.2 22.9 %copy-start = (bf16[256,1024]{1,0:T(8,128)(2,1)S(1)}, bf16[256,1024]{1,0:T(8,128)(2,1)}, u32[]{:S(2)}) copy-start(bf16[256,1024]{1,0:T(8,128)(2,1)} %qo.5) | copy-start | bytes 1572868
  7.2 22.9 %copy-start.1 = (bf16[256,1024]{1,0:T(8,128)(2,1)S(1)}, bf16[256,1024]{1,0:T(8,128)(2,1)}, u32[]{:S(2)}) copy-start(bf16[256,1024]{1,0:T(8,128)(2,1)} %ko.5) | copy-start | bytes 1572868
  7.2 22.9 %copy-start.2 = (bf16[256,1024]{1,0:T(8,128)(2,1)S(1)}, bf16[256,1024]{1,0:T(8,128)(2,1)}, u32[]{:S(2)}) copy-start(bf16[256,1024]{1,0:T(8,128)(2,1)} %vo.3) | copy-start | bytes 1572868
  7.2 5.3 %copy-start.20 = (s32[12]{0:T(128)S(1)}, s32[12]{0:T(128)}, u32[]{:S(2)}) copy-start(s32[12]{0:T(128)} %param.10) | copy-start | bytes 148
  7.2 75.3 %all-gather.3.cloned.1.call-start = ((), (), s32[]{:S(2)}) async-start(), calls=%async_computation.2 | async-start | bytes 2621440 | tf_op jit(solution)/shard_map/all_gather | solution.py:304
  9.5 20.5 %collective-permute-start = (bf16[3,256,512]{2,1,0:T(8,128)(2,1)S(1)}, bf16[3,256,512]{2,1,0:T(8,128)(2,1)S(1)}, u32[]{:S(2)}, u32[]{:S(2)}) collective-permute-start(bf16[3,256,512]{2,1,0:T(8,128)(2,1)S(1)} %pad_maximum_fusion.2), channel_id=1, source_target_pairs={{0,16},{16,0},{1,17},{17,1},{2,18},{18,2},{3,19},{19,3},{4,20},{20... | collective-permute-start | bytes 2359304 | tf_op jit(solution)/shard_map/ppermute | solution.py:268
  30.1 4.9 %copy-start.15 = (bf16[256,1536]{1,0:T(8,128)(2,1)S(1)}, bf16[256,1536]{1,0:T(8,128)(2,1)}, u32[]{:S(2)}) copy-start(bf16[256,1536]{1,0:T(8,128)(2,1)} %param.11) | copy-start | bytes 2359300
  34.9 92.5 %reduce-scatter.2.cloned.1.call-start = ((), (), s32[]{:S(2)}) async-start(), calls=%async_computation.1 | async-start | bytes 2621440 | tf_op jit(solution)/shard_map/reduce_scatter | solution.py:297
  35.0 20.5 %collective-permute-start.3 = (bf16[256,1536]{1,0:T(8,128)(2,1)S(1)}, bf16[256,1536]{1,0:T(8,128)(2,1)S(1)}, u32[]{:S(2)}, u32[]{:S(2)}) collective-permute-start(bf16[256,1536]{1,0:T(8,128)(2,1)S(1)} %copy-done.15), channel_id=1, source_target_pairs={{0,16},{16,0},{1,17},{17,1},{2,18},{18,2},{3,19},{19,3},{4,20},{20... | collective-permute-start | bytes 2359304 | tf_op jit(solution)/shard_map/ppermute | solution.py:268
  40.1 15.5 %copy-start.4 = (bf16[2,1,512,1536]{3,2,1,0:T(8,128)(2,1)}, bf16[2,1,512,1536]{3,2,1,0:T(8,128)(2,1)S(1)}, u32[]{:S(2)}) copy-start(bf16[2,1,512,1536]{3,2,1,0:T(8,128)(2,1)S(1)} %get-tuple-element.15) | copy-start | bytes 9437188
  40.1 19.0 %copy-start.7 = (bf16[2,1,512,1536]{3,2,1,0:T(8,128)(2,1)}, bf16[2,1,512,1536]{3,2,1,0:T(8,128)(2,1)S(1)}, u32[]{:S(2)}) copy-start(bf16[2,1,512,1536]{3,2,1,0:T(8,128)(2,1)S(1)} %get-tuple-element.16) | copy-start | bytes 9437188
  42.4 16.7 %copy-start.16 = (bf16[256,1536]{1,0:T(8,128)(2,1)S(1)}, bf16[256,1536]{1,0:T(8,128)(2,1)}, u32[]{:S(2)}) copy-start(bf16[256,1536]{1,0:T(8,128)(2,1)} %param.11) | copy-start | bytes 2359300
  42.4 35.0 %collective-permute-start.5 = (bf16[256,1024]{1,0:T(8,128)(2,1)}, bf16[256,1024]{1,0:T(8,128)(2,1)}, u32[]{:S(2)}, u32[]{:S(2)}) collective-permute-start(bf16[256,1024]{1,0:T(8,128)(2,1)} %fusion.39), channel_id=1, source_target_pairs={{0,16},{16,0},{1,17},{17,1},{2,18},{18,2},{3,19},{19,3},{4,20},{20... | collective-permute-start | bytes 1572872 | tf_op jit(solution)/shard_map/ppermute | solution.py:268
  55.5 3.5 %copy-start.18 = (bf16[256,1536]{1,0:T(8,128)(2,1)}, bf16[256,1536]{1,0:T(8,128)(2,1)S(1)}, u32[]{:S(2)}) copy-start(bf16[256,1536]{1,0:T(8,128)(2,1)S(1)} %collective-permute-done.3) | copy-start | bytes 2359300
  57.3 19.0 %collective-permute-start.4 = (bf16[256,1024]{1,0:T(8,128)(2,1)}, bf16[256,1024]{1,0:T(8,128)(2,1)}, u32[]{:S(2)}, u32[]{:S(2)}) collective-permute-start(bf16[256,1024]{1,0:T(8,128)(2,1)} %convolution_convert_fusion.2), channel_id=1, source_target_pairs={{0,16},{16,0},{1,17},{17,1},{2,18},{18,2},{3,19},{19,3},{4,20},{20... | collective-permute-start | bytes 1572872 | tf_op jit(solution)/shard_map/ppermute | solution.py:268
  84.8 25.2 %collective-permute-start.1 = (bf16[2,512,512]{2,1,0:T(8,128)(2,1)}, bf16[2,512,512]{2,1,0:T(8,128)(2,1)}, u32[]{:S(2)}, u32[]{:S(2)}) collective-permute-start(bf16[2,512,512]{2,1,0:T(8,128)(2,1)} %constant_dynamic-slice_fusion.1), channel_id=1, source_target_pairs={{0,16},{16,0},{1,17},{17,1},{2,18},{18,2},{3,19},{19,3},{4,20},{20... | collective-permute-start | bytes 3145736 | tf_op jit(solution)/shard_map/ppermute | solution.py:268
  86.3 3.9 %copy-start.8 = (bf16[2,1,512,1536]{3,2,1,0:T(8,128)(2,1)S(1)}, bf16[2,1,512,1536]{3,2,1,0:T(8,128)(2,1)}, u32[]{:S(2)}) copy-start(bf16[2,1,512,1536]{3,2,1,0:T(8,128)(2,1)} %copy-done.7) | copy-start | bytes 9437188
  86.3 3.9 %copy-start.10 = (bf16[2048,512]{1,0:T(8,128)(2,1)S(1)}, bf16[2048,512]{1,0:T(8,128)(2,1)}, u32[]{:S(2)}) copy-start(bf16[2048,512]{1,0:T(8,128)(2,1)} %all-gather.3.cloned.1.call-done) | copy-start | bytes 6291460
  92.3 17.7 %copy-start.5 = (bf16[2,1,512,1536]{3,2,1,0:T(8,128)(2,1)S(1)}, bf16[2,1,512,1536]{3,2,1,0:T(8,128)(2,1)}, u32[]{:S(2)}) copy-start(bf16[2,1,512,1536]{3,2,1,0:T(8,128)(2,1)} %copy-done.4) | copy-start | bytes 9437188
  113.0 28.2 %collective-permute-start.2 = (bf16[256,1536]{1,0:T(8,128)(2,1)}, bf16[256,1536]{1,0:T(8,128)(2,1)S(1)}, u32[]{:S(2)}, u32[]{:S(2)}) collective-permute-start(bf16[256,1536]{1,0:T(8,128)(2,1)} %fusion.29), channel_id=1, source_target_pairs={{0,16},{16,0},{1,17},{17,1},{2,18},{18,2},{3,19},{19,3},{4,20},{20... | collective-permute-start | bytes 2359304 | tf_op jit(solution)/shard_map/ppermute | solution.py:268
  127.5 1.0 copy-start.3
  128.5 7.2 %copy-start.11 = (bf16[2,1,256,512]{3,2,0,1:T(8,128)(2,1)S(1)}, bf16[2,1,256,512]{3,2,0,1:T(8,128)(2,1)}, u32[]{:S(2)}) copy-start(bf16[2,1,256,512]{3,2,0,1:T(8,128)(2,1)} %get-tuple-element.17) | copy-start | bytes 1572868
  128.5 7.2 %copy-start.12 = (bf16[2,1,256,512]{3,2,0,1:T(8,128)(2,1)S(1)}, bf16[2,1,256,512]{3,2,0,1:T(8,128)(2,1)}, u32[]{:S(2)}) copy-start(bf16[2,1,256,512]{3,2,0,1:T(8,128)(2,1)} %get-tuple-element.18) | copy-start | bytes 1572868
  128.5 7.2 %copy-start.13 = (bf16[2,1,256,512]{3,2,0,1:T(8,128)(2,1)S(1)}, bf16[2,1,256,512]{3,2,0,1:T(8,128)(2,1)}, u32[]{:S(2)}) copy-start(bf16[2,1,256,512]{3,2,0,1:T(8,128)(2,1)} %get-tuple-element.19) | copy-start | bytes 1572868
  128.5 7.2 %copy-start.14 = (bf16[2,1,256,512]{3,2,0,1:T(8,128)(2,1)S(1)}, bf16[2,1,256,512]{3,2,0,1:T(8,128)(2,1)}, u32[]{:S(2)}) copy-start(bf16[2,1,256,512]{3,2,0,1:T(8,128)(2,1)} %get-tuple-element.20) | copy-start | bytes 1572868
  128.5 7.2 %copy-start.17 = (bf16[256,1536]{1,0:T(8,128)(2,1)S(1)}, bf16[256,1536]{1,0:T(8,128)(2,1)}, u32[]{:S(2)}) copy-start(bf16[256,1536]{1,0:T(8,128)(2,1)} %param.11) | copy-start | bytes 2359300
  128.5 7.2 %copy-start.19 = (bf16[256,1536]{1,0:T(8,128)(2,1)S(1)}, bf16[256,1536]{1,0:T(8,128)(2,1)}, u32[]{:S(2)}) copy-start(bf16[256,1536]{1,0:T(8,128)(2,1)} %copy-done.18) | copy-start | bytes 2359300
  134.2 19.2 %collective-permute-start.6 = (bf16[3,256,512]{2,1,0:T(8,128)(2,1)S(1)}, bf16[3,256,512]{2,1,0:T(8,128)(2,1)S(1)}, u32[]{:S(2)}, u32[]{:S(2)}) collective-permute-start(bf16[3,256,512]{2,1,0:T(8,128)(2,1)S(1)} %get-tuple-element.12), channel_id=1, source_target_pairs={{0,16},{16,0},{1,17},{17,1},{2,18},{18,2},{3,19},{19,3},{4,20},{20... | collective-permute-start | bytes 2359304 | tf_op jit(solution)/shard_map/ppermute | solution.py:268
  135.7 5.4 %copy-start.6 = (bf16[2,1,512,1536]{3,2,1,0:T(8,128)(2,1)S(1)}, bf16[2,1,512,1536]{3,2,1,0:T(8,128)(2,1)}, u32[]{:S(2)}) copy-start(bf16[2,1,512,1536]{3,2,1,0:T(8,128)(2,1)} %copy-done.4) | copy-start | bytes 9437188
  135.7 5.4 %copy-start.9 = (f32[256,1536]{1,0:T(8,128)S(1)}, f32[256,1536]{1,0:T(8,128)}, u32[]{:S(2)}) copy-start(f32[256,1536]{1,0:T(8,128)} %fusion.8) | copy-start | bytes 4718596
Sparse Core Ops, SparseCore 0:
  35.1 47.4 all-gather.2
  84.8 42.6 reduce-scatter.1
